TPU v7x, 32 devices: a whole 2x2x4 slice. The times are simulated.
32 devices in a mesh: gy: 4 (over z), gx: 8 (over y, x, core).
Axes of the slice: x: 2, y: 2, z: 4, core: 2. Of those that a mesh axis runs over, the one named last changes fastest.
Arguments:
- field: bfloat16 [256, 128, 128], P('gy', 'gx'), may hold values from -8 to 8
- cotangent: bfloat16 [128, 64, 256], P('gy', 'gx'), may hold values from -6 to 6
- gain_fine: float32 [128], replicated, may hold values from 0.1 to 1.9
- weight_fine: bfloat16 [3, 3, 128, 128], replicated, may hold values from -0.1875 to 0.1875
- projection: bfloat16 [128, 256], replicated, may hold values from -0.5 to 0.5
- gain_coarse: float32 [256], replicated, may hold values from 0.1 to 1.9
- weight_coarse: bfloat16 [3, 3, 256, 256], replicated, may hold values from -0.125 to 0.125
Outputs:
- coarse_output: bfloat16 [128, 64, 256], P('gy', 'gx')
- field_grad: bfloat16 [256, 128, 128], P('gy', 'gx')
- fine_weight_grad: float32 [3, 3, 128, 128], replicated
- fine_gain_grad: float32 [128], replicated
- projection_grad: float32 [128, 256], replicated
- coarse_weight_grad: float32 [3, 3, 256, 256], replicated
- coarse_gain_grad: float32 [256], replicated
All inputs are finite; a program needn't handle non-finite values.
Results may differ from a plain program's by a relative error of at most 0.014.
Values may be sent and summed in bfloat16 or wider, within the bound.
A program may use at most 64 MiB of HBM per device.

v0:
```python
import jax
import jax.numpy as jnp
from jax import lax
from jax.sharding import PartitionSpec as P

GROUPS = 32


EPSILON = 1e-05


def extended(cells, sides, width):
    for axis, dim in sides:
        count = lax.axis_size(axis)
        ends = count - 1
        head = lax.slice_in_dim(cells, 0, width, axis=dim)
        tail = lax.slice_in_dim(cells, cells.shape[dim] - width, cells.shape[dim], axis=dim)
        cells = jnp.concatenate(
            [
                lax.ppermute(tail, axis, [(i, (i + 1) % count) for i in range(ends)]),
                cells,
                lax.ppermute(head, axis, [((i + 1) % count, i) for i in range(ends)]),
            ],
            axis=dim,
        )
    return cells


def conv_forward(padded, weight, height, width):
    channels = padded.shape[2]
    total = jnp.zeros((height * width, weight.shape[3]), jnp.float32)
    for row_tap in range(3):
        for col_tap in range(3):
            window = padded[row_tap : row_tap + height, col_tap : col_tap + width].reshape(
                height * width, channels
            )
            total = total + jnp.dot(
                window, weight[row_tap, col_tap], preferred_element_type=jnp.float32
            )
    return total.reshape(height, width, weight.shape[3])


def conv_transpose(padded, weight, height, width):
    channels = padded.shape[2]
    total = jnp.zeros((height * width, weight.shape[2]), jnp.float32)
    for row_tap in range(3):
        for col_tap in range(3):
            window = padded[
                2 - row_tap : 2 - row_tap + height, 2 - col_tap : 2 - col_tap + width
            ].reshape(height * width, channels)
            total = total + jnp.dot(
                window, weight[row_tap, col_tap].T, preferred_element_type=jnp.float32
            )
    return total.reshape(height, width, weight.shape[2])


def conv_weight(padded, grads, height, width):
    channels = padded.shape[2]
    flat_grads = grads.reshape(height * width, grads.shape[2])
    taps = []
    for row_tap in range(3):
        for col_tap in range(3):
            window = padded[row_tap : row_tap + height, col_tap : col_tap + width].reshape(
                height * width, channels
            )
            taps.append(
                lax.dot_general(
                    window, flat_grads, (((0,), (0,)), ((), ())), preferred_element_type=jnp.float32
                )
            )
    return jnp.stack(taps).reshape(3, 3, channels, grads.shape[2])


def tile_rims(values):
    return extended(values, (("gy", 0), ("gx", 1)), 1)


def upsample(values):
    rows, cols, channels = values.shape
    return jnp.broadcast_to(values[:, None, :, None, :], (rows, 2, cols, 2, channels)).reshape(
        2 * rows, 2 * cols, channels
    )


def global_sums(pair):
    return lax.psum((pair[0], pair[1]), ("gy", "gx"))


def normalize(values, count):
    channels = values.shape[2]
    grouped = values.reshape(-1, GROUPS, channels // GROUPS)
    first, second = global_sums(
        (jnp.sum(grouped, axis=(0, 2)), jnp.sum(grouped * grouped, axis=(0, 2)))
    )
    average = first / count
    variance = second / count - average * average
    inverse = lax.rsqrt(variance + EPSILON)
    normed = (grouped - average[None, :, None]) * inverse[None, :, None]
    return (normed.reshape(values.shape), inverse)


def norm_backward(dnorm, normed, inverse, count):
    channels = normed.shape[2]
    dgroup = dnorm.reshape(-1, GROUPS, channels // GROUPS)
    ngroup = normed.reshape(-1, GROUPS, channels // GROUPS)
    first, second = global_sums(
        (jnp.sum(dgroup, axis=(0, 2)), jnp.sum(dgroup * ngroup, axis=(0, 2)))
    )
    result = inverse[None, :, None] * (
        dgroup - (first / count)[None, :, None] - ngroup * (second / count)[None, :, None]
    )
    return result.reshape(normed.shape)


def silu_slope(act):
    sigma = jax.nn.sigmoid(act)
    return sigma * (1.0 + act * (1.0 - sigma))


def on_device(field, cotangent, gain_fine, weight_fine, projection, gain_coarse, weight_coarse):
    height, width, chan_fine = field.shape
    chan_coarse = projection.shape[1]
    half_h, half_w = (height // 2, width // 2)
    cells_all = height * width * lax.axis_size("gy") * lax.axis_size("gx")
    fine_count = cells_all * (chan_fine // GROUPS)
    coarse_count = cells_all // 4 * (chan_coarse // GROUPS)
    values = field.astype(jnp.float32)
    normed_fine, inverse_fine = normalize(values, fine_count)
    act_fine = normed_fine * gain_fine
    hidden_fine = jax.nn.silu(act_fine).astype(jnp.bfloat16)
    padded_fine = tile_rims(hidden_fine)
    block_fine = (values + conv_forward(padded_fine, weight_fine, height, width)).astype(
        jnp.bfloat16
    )
    pooled = jnp.mean(
        block_fine.astype(jnp.float32).reshape(half_h, 2, half_w, 2, chan_fine), axis=(1, 3)
    ).astype(jnp.bfloat16)
    coarse_in = (
        jnp.dot(pooled.reshape(-1, chan_fine), projection, preferred_element_type=jnp.float32)
        .reshape(half_h, half_w, chan_coarse)
        .astype(jnp.bfloat16)
    )
    coarse_vals = coarse_in.astype(jnp.float32)
    normed_coarse, inverse_coarse = normalize(coarse_vals, coarse_count)
    act_coarse = normed_coarse * gain_coarse
    hidden_coarse = jax.nn.silu(act_coarse).astype(jnp.bfloat16)
    padded_coarse = tile_rims(hidden_coarse)
    coarse_output = (
        coarse_vals + conv_forward(padded_coarse, weight_coarse, half_h, half_w)
    ).astype(jnp.bfloat16)
    padded_grad = tile_rims(cotangent)
    coarse_weight_grad = conv_weight(padded_coarse, cotangent, half_h, half_w)
    dact_coarse = conv_transpose(padded_grad, weight_coarse, half_h, half_w) * silu_slope(
        act_coarse
    )
    coarse_gain_grad = jnp.sum((dact_coarse * normed_coarse).reshape(-1, chan_coarse), axis=0)
    dcoarse = (
        cotangent.astype(jnp.float32)
        + norm_backward(dact_coarse * gain_coarse, normed_coarse, inverse_coarse, coarse_count)
    ).astype(jnp.bfloat16)
    projection_grad = lax.dot_general(
        pooled.reshape(-1, chan_fine),
        dcoarse.reshape(-1, chan_coarse),
        (((0,), (0,)), ((), ())),
        preferred_element_type=jnp.float32,
    )
    dpool = jnp.dot(
        dcoarse.reshape(-1, chan_coarse), projection.T, preferred_element_type=jnp.float32
    ).reshape(half_h, half_w, chan_fine)
    small_dblock = (dpool * 0.25).astype(jnp.bfloat16)
    dblock = upsample(small_dblock)
    padded_dblock = tile_rims(dblock)
    fine_weight_grad = conv_weight(padded_fine, dblock, height, width)
    dact_fine = conv_transpose(padded_dblock, weight_fine, height, width) * silu_slope(act_fine)
    fine_gain_grad = jnp.sum((dact_fine * normed_fine).reshape(-1, chan_fine), axis=0)
    field_grad = (
        dblock.astype(jnp.float32)
        + norm_backward(dact_fine * gain_fine, normed_fine, inverse_fine, fine_count)
    ).astype(jnp.bfloat16)
    fine_weight_grad, fine_gain_grad, projection_grad, coarse_weight_grad, coarse_gain_grad = (
        lax.psum(
            (
                fine_weight_grad,
                fine_gain_grad,
                projection_grad,
                coarse_weight_grad,
                coarse_gain_grad,
            ),
            ("gy", "gx"),
        )
    )
    return (
        coarse_output,
        field_grad,
        fine_weight_grad,
        fine_gain_grad,
        projection_grad,
        coarse_weight_grad,
        coarse_gain_grad,
    )


def solution(mesh):
    return jax.shard_map(
        on_device,
        mesh=mesh,
        in_specs=(P("gy", "gx", None), P("gy", "gx", None), P(), P(), P(), P(), P()),
        out_specs=(P("gy", "gx", None), P("gy", "gx", None), P(), P(), P(), P(), P()),
        check_vma=False,
    )
```

profile of v0, /device:TPU:0, one launch (start us, length us, event | category | flops | bytes accessed | tf_op | source)
XLA Modules:
  0.0 403.1 jit_solution(8453528038694597793)
XLA Ops:
  7.2 0.7 fusion.213
  7.9 1.3 collective-permute-start.9
  9.2 1.1 convert_reduce_fusion
  10.8 5.6 %collective-permute-start.8 = (bf16[1,8,256]{2,1,0:T(8,128)(2,1)S(1)}, bf16[1,8,256]{2,1,0:T(8,128)(2,1)S(1)}, u32[]{:S(2)}, u32[]{:S(2)}) collective-permute-start(bf16[1,8,256]{2,1,0:T(8,128)(2,1)S(1)} %get-tuple-element.68), channel_id=1, source_target_pairs={{0,8},{8,16},{16,24},{1,9},{9,17},{17,25},{2,10},{10,18},{18,26},{... | collective-permute-start | bytes 12296 | tf_op jit(solution)/shard_map/ppermute | solution.py:20
  16.3 40.9 %all-reduce.3 = (f32[32]{0:T(128)S(1)}, f32[32]{0:T(128)S(1)}) all-reduce(f32[32]{0:T(128)S(1)} %reduce_sum.127, f32[32]{0:T(128)S(1)} %reduce_sum.121), channel_id=1, replica_groups=mesh['gy'=4,'gx'=8] {'gy','gx'}, use_global_device_ids=true, to_apply=%region_5.6 | all-reduce | flops 64 | bytes 512 | tf_op jit(solution)/shard_map/psum | solution.py:86
  57.7 1.1 fusion.41
  58.8 2.2 collective-permute-start
  61.0 1.3 collective-permute-start.1
  62.3 1.0 constant_dynamic-update-slice_fusion.1
  63.4 1.3 collective-permute-start.10
  64.7 3.0 collective-permute-start.11
  67.9 3.8 collective-permute-start.2
  71.7 1.3 collective-permute-start.3
  73.3 0.9 fusion.83
  74.2 0.6 collective-permute-done.3
  74.8 0.3 maximum_maximum_fusion
  77.2 0.7 copy-done.1
  78.0 0.4 convert_reduce_fusion.1
  78.5 0.6 copy-done.14
  79.7 0.9 fusion.76
  80.7 43.3 %all-reduce.2 = (f32[32]{0:T(128)S(1)}, f32[32]{0:T(128)S(1)}) all-reduce(f32[32]{0:T(128)S(1)} %reduce_sum.140, f32[32]{0:T(128)S(1)} %reduce_sum.134), channel_id=1, replica_groups=mesh['gy'=4,'gx'=8] {'gy','gx'}, use_global_device_ids=true, to_apply=%region_12.13 | all-reduce | flops 64 | bytes 512 | tf_op jit(solution)/shard_map/psum | solution.py:86
  124.3 1.2 convolution_add_fusion.19
  126.7 0.2 copy-done.19
  126.9 1.0 multiply_reduce_fusion.1
  128.3 40.3 %all-reduce.1 = (f32[32]{0:T(128)S(1)}, f32[32]{0:T(128)S(1)}) all-reduce(f32[32]{0:T(128)S(1)} %reduce_sum.173, f32[32]{0:T(128)S(1)} %reduce_sum.170), channel_id=1, replica_groups=mesh['gy'=4,'gx'=8] {'gy','gx'}, use_global_device_ids=true, to_apply=%region_18.19 | all-reduce | flops 64 | bytes 512 | tf_op jit(solution)/shard_map/psum | solution.py:86
  169.0 1.1 add_convert_fusion
  170.1 1.8 convolution_bitcast_fusion.9
  172.1 2.1 collective-permute-start.4
  174.2 1.3 collective-permute-start.5
  175.7 4.5 %collective-permute-start.12 = (bf16[1,16,128]{2,1,0:T(8,128)(2,1)S(1)}, bf16[1,16,128]{2,1,0:T(8,128)(2,1)S(1)}, u32[]{:S(2)}, u32[]{:S(2)}) collective-permute-start(bf16[1,16,128]{2,1,0:T(8,128)(2,1)S(1)} %get-tuple-element.55), channel_id=1, source_target_pairs={{0,8},{8,16},{16,24},{1,9},{9,17},{17,25},{2,10},{10,18},{18,26},{... | collective-permute-start | bytes 12296 | tf_op jit(solution)/shard_map/ppermute | solution.py:20
  180.3 1.3 collective-permute-start.13
  181.6 1.2 fusion.29
  182.8 0.3 fusion.28
  183.1 0.3 fusion.27
  183.4 0.3 fusion.26
  183.6 0.3 fusion.25
  183.9 0.3 fusion.24
  184.2 0.3 fusion.23
  184.5 0.3 fusion.22
  184.7 0.3 fusion.21
  185.1 1.3 collective-permute-start.6
  186.4 1.3 collective-permute-start.7
  187.8 1.3 collective-permute-start.14
  189.1 6.3 %collective-permute-start.15 = (bf16[66,1,128]{2,1,0:T(2,128)(2,1)S(1)}, bf16[66,1,128]{2,1,0:T(2,128)(2,1)S(1)}, u32[]{:S(2)}, u32[]{:S(2)}) collective-permute-start(bf16[66,1,128]{2,1,0:T(2,128)(2,1)S(1)} %get-tuple-element.46), channel_id=1, source_target_pairs={{0,1},{1,2},{2,3},{3,4},{4,5},{5,6},{6,7},{8,9},{9,10},{10,11},{11... | collective-permute-start | bytes 50696 | tf_op jit(solution)/shard_map/ppermute | solution.py:20
  195.7 0.9 fusion.88
  196.6 0.3 pad_maximum_fusion.1
  198.3 0.2 convolution_add_fusion.2
  198.5 0.2 convolution_add_fusion.1
  198.8 0.2 fusion.1
  199.0 0.4 copy-done.22
  199.4 0.4 fusion.50
  200.2 43.8 %all-reduce = (f32[32]{0:T(128)S(1)}, f32[32]{0:T(128)S(1)}, f32[128]{0:T(128)}, f32[256]{0:T(256)}) all-reduce(f32[32]{0:T(128)S(1)} %reduce_sum.179, f32[32]{0:T(128)S(1)} %reduce_sum.176, f32[128]{0:T(128)S(1)} %get-tuple-element.7, f32[256]{0:T(256)S(1)} %get-tuple-element.9), channel_id=1, replica_groups=mesh['gy'=4,'gx'=8] {'gy','gx'}, use_global_device_ids=true, to_apply=%region_24.25 | all-reduce | flops 448 | bytes 3584 | tf_op jit(solution)/shard_map/psum | solution.py:86
  244.4 0.9 fusion.49
  245.7 0.7 copy-done.17
  246.9 0.2 fusion.15
  247.6 0.2 fusion.12
  248.3 0.2 fusion.10
  248.5 1.4 copy-done.4
  251.1 0.4 copy-done.13
  251.5 0.9 fusion.18
  252.3 138.1 %all-reduce.7.cloned.1.call-done = (f32[3,3,128,128]{3,2,1,0:T(8,128)}, f32[128,256]{1,0:T(8,128)}, f32[3,3,256,256]{3,2,1,0:T(8,128)}) async-done(((f32[3,3,128,128]{3,2,1,0:T(8,128)}, f32[128,256]{1,0:T(8,128)}, f32[3,3,256,256]{3,2,1,0:T(8,128)}), (f32[3,3,128,128]{3,2,1,0:T(8,128)}, f32[128,256]{1,0:T(8,128)}, f32[3,3,256,256]{3,2,1,0:T(8,128)})) %all-reduce.7.cloned.1.call-update) | async-done | bytes 3080208 | tf_op jit(solution)/shard_map/psum | solution.py:181
  390.4 2.0 copy.95
  392.3 0.7 copy.96
  393.0 3.2 copy.97
  (150 shorter events, 11.9 us)
Async XLA Ops:
  7.2 71.9 %copy-start = (bf16[128,256]{1,0:T(8,128)(2,1)S(1)}, bf16[128,256]{1,0:T(8,128)(2,1)}, u32[]{:S(2)}) copy-start(bf16[128,256]{1,0:T(8,128)(2,1)} %param.11) | copy-start | bytes 196612
  7.2 383.2 %all-reduce.7.cloned.1.call-start = ((), (), s32[]{:S(2)}) async-start(), calls=%async_computation | async-start | bytes 6160384 | tf_op jit(solution)/shard_map/psum | solution.py:181
  7.9 55.4 %collective-permute-start.9 = (bf16[1,8,256]{2,1,0:T(8,128)(2,1)S(1)}, bf16[1,8,256]{2,1,0:T(8,128)(2,1)S(1)}, u32[]{:S(2)}, u32[]{:S(2)}) collective-permute-start(bf16[1,8,256]{2,1,0:T(8,128)(2,1)S(1)} %get-tuple-element.67), channel_id=1, source_target_pairs={{8,0},{16,8},{24,16},{9,1},{17,9},{25,17},{10,2},{18,10},{26,18},{... | collective-permute-start | bytes 12296 | tf_op jit(solution)/shard_map/ppermute | solution.py:22
  10.3 62.7 %copy-start.15 = (bf16[3,3,128,128]{3,2,1,0:T(8,128)(2,1)S(1)}, bf16[3,3,128,128]{3,2,1,0:T(8,128)(2,1)}, u32[]{:S(2)}) copy-start(bf16[3,3,128,128]{3,2,1,0:T(8,128)(2,1)} %param.10) | copy-start | bytes 884740
  10.8 51.5 %collective-permute-start.8 = (bf16[1,8,256]{2,1,0:T(8,128)(2,1)S(1)}, bf16[1,8,256]{2,1,0:T(8,128)(2,1)S(1)}, u32[]{:S(2)}, u32[]{:S(2)}) collective-permute-start(bf16[1,8,256]{2,1,0:T(8,128)(2,1)S(1)} %get-tuple-element.68), channel_id=1, source_target_pairs={{0,8},{8,16},{16,24},{1,9},{9,17},{17,25},{2,10},{10,18},{18,26},{... | collective-permute-start | bytes 12296 | tf_op jit(solution)/shard_map/ppermute | solution.py:20
  57.7 5.7 %copy-start.21 = (f32[128]{0:T(128)}, f32[128]{0:T(128)S(1)}, u32[]{:S(2)}) copy-start(f32[128]{0:T(128)S(1)} %mul.159) | copy-start | bytes 1540
  58.8 9.0 %collective-permute-start = (bf16[1,16,128]{2,1,0:T(8,128)(2,1)S(1)}, bf16[1,16,128]{2,1,0:T(8,128)(2,1)S(1)}, u32[]{:S(2)}, u32[]{:S(2)}) collective-permute-start(bf16[1,16,128]{2,1,0:T(8,128)(2,1)S(1)} %get-tuple-element.59), channel_id=1, source_target_pairs={{0,8},{8,16},{16,24},{1,9},{9,17},{17,25},{2,10},{10,18},{18,26},{... | collective-permute-start | bytes 12296 | tf_op jit(solution)/shard_map/ppermute | solution.py:20
  61.0 6.8 %collective-permute-start.1 = (bf16[1,16,128]{2,1,0:T(8,128)(2,1)S(1)}, bf16[1,16,128]{2,1,0:T(8,128)(2,1)S(1)}, u32[]{:S(2)}, u32[]{:S(2)}) collective-permute-start(bf16[1,16,128]{2,1,0:T(8,128)(2,1)S(1)} %get-tuple-element.60), channel_id=1, source_target_pairs={{8,0},{16,8},{24,16},{9,1},{17,9},{25,17},{10,2},{18,10},{26,18},{... | collective-permute-start | bytes 12296 | tf_op jit(solution)/shard_map/ppermute | solution.py:22
  62.3 10.9 %copy-start.2 = (bf16[3,3,256,256]{3,2,1,0:T(8,128)(2,1)S(1)}, bf16[3,3,256,256]{3,2,1,0:T(8,128)(2,1)}, u32[]{:S(2)}) copy-start(bf16[3,3,256,256]{3,2,1,0:T(8,128)(2,1)} %param.13) | copy-start | bytes 3538948
  62.3 10.9 %copy-start.3 = (bf16[32,8,256]{2,1,0:T(8,128)(2,1)S(1)}, bf16[32,8,256]{2,1,0:T(8,128)(2,1)}, u32[]{:S(2)}) copy-start(bf16[32,8,256]{2,1,0:T(8,128)(2,1)} %param.8) | copy-start | bytes 393220
  63.4 60.8 %collective-permute-start.10 = (bf16[34,1,256]{2,1,0:T(2,128)(2,1)S(1)}, bf16[34,1,256]{2,1,0:T(2,128)(2,1)S(1)}, u32[]{:S(2)}, u32[]{:S(2)}) collective-permute-start(bf16[34,1,256]{2,1,0:T(2,128)(2,1)S(1)} %get-tuple-element.61), channel_id=1, source_target_pairs={{1,0},{2,1},{3,2},{4,3},{5,4},{6,5},{7,6},{9,8},{10,9},{11,10},{12... | collective-permute-start | bytes 52232 | tf_op jit(solution)/shard_map/ppermute | solution.py:22
  64.7 60.7 %collective-permute-start.11 = (bf16[34,1,256]{2,1,0:T(2,128)(2,1)S(1)}, bf16[34,1,256]{2,1,0:T(2,128)(2,1)S(1)}, u32[]{:S(2)}, u32[]{:S(2)}) collective-permute-start(bf16[34,1,256]{2,1,0:T(2,128)(2,1)S(1)} %get-tuple-element.62), channel_id=1, source_target_pairs={{0,1},{1,2},{2,3},{3,4},{4,5},{5,6},{6,7},{8,9},{9,10},{10,11},{11... | collective-permute-start | bytes 52232 | tf_op jit(solution)/shard_map/ppermute | solution.py:20
  67.9 6.3 %collective-permute-start.2 = (bf16[66,1,128]{2,1,0:T(2,128)(2,1)S(1)}, bf16[66,1,128]{2,1,0:T(2,128)(2,1)S(1)}, u32[]{:S(2)}, u32[]{:S(2)}) collective-permute-start(bf16[66,1,128]{2,1,0:T(2,128)(2,1)S(1)} %get-tuple-element.49), channel_id=1, source_target_pairs={{0,1},{1,2},{2,3},{3,4},{4,5},{5,6},{6,7},{8,9},{9,10},{10,11},{11... | collective-permute-start | bytes 50696 | tf_op jit(solution)/shard_map/ppermute | solution.py:20
  71.7 3.1 collective-permute-start.3
  75.3 0.7 copy-start.9
  75.3 0.8 copy-start.11
  75.3 0.8 copy-start.7
  75.3 1.3 copy-start.5
  77.0 1.0 copy-start.1
  78.4 0.7 copy-start.14
  79.3 89.7 %copy-start.12 = (f32[32,8,256]{2,1,0:T(8,128)}, f32[32,8,256]{2,1,0:T(8,128)S(1)}, u32[]{:S(2)}) copy-start(f32[32,8,256]{2,1,0:T(8,128)S(1)} %get-tuple-element.75) | copy-start | bytes 786436
  125.9 1.0 copy-start.19
  126.0 0.9 copy-start.24
  170.1 13.0 %copy-start.10 = (bf16[64,16,128]{2,1,0:T(8,128)(2,1)S(1)}, bf16[64,16,128]{2,1,0:T(8,128)(2,1)}, u32[]{:S(2)}) copy-start(bf16[64,16,128]{2,1,0:T(8,128)(2,1)} %copy-done.9) | copy-start | bytes 786436
  171.9 11.4 %copy-start.8 = (bf16[64,16,128]{2,1,0:T(8,128)(2,1)S(1)}, bf16[64,16,128]{2,1,0:T(8,128)(2,1)}, u32[]{:S(2)}) copy-start(bf16[64,16,128]{2,1,0:T(8,128)(2,1)} %copy-done.7) | copy-start | bytes 786436
  172.1 12.9 %collective-permute-start.4 = (bf16[1,8,256]{2,1,0:T(8,128)(2,1)S(1)}, bf16[1,8,256]{2,1,0:T(8,128)(2,1)S(1)}, u32[]{:S(2)}, u32[]{:S(2)}) collective-permute-start(bf16[1,8,256]{2,1,0:T(8,128)(2,1)S(1)} %get-tuple-element.69), channel_id=1, source_target_pairs={{0,8},{8,16},{16,24},{1,9},{9,17},{17,25},{2,10},{10,18},{18,26},{... | collective-permute-start | bytes 12296 | tf_op jit(solution)/shard_map/ppermute | solution.py:20
  174.2 10.8 %collective-permute-start.5 = (bf16[1,8,256]{2,1,0:T(8,128)(2,1)S(1)}, bf16[1,8,256]{2,1,0:T(8,128)(2,1)S(1)}, u32[]{:S(2)}, u32[]{:S(2)}) collective-permute-start(bf16[1,8,256]{2,1,0:T(8,128)(2,1)S(1)} %get-tuple-element.70), channel_id=1, source_target_pairs={{8,0},{16,8},{24,16},{9,1},{17,9},{25,17},{10,2},{18,10},{26,18},{... | collective-permute-start | bytes 12296 | tf_op jit(solution)/shard_map/ppermute | solution.py:22
  175.7 12.0 %collective-permute-start.12 = (bf16[1,16,128]{2,1,0:T(8,128)(2,1)S(1)}, bf16[1,16,128]{2,1,0:T(8,128)(2,1)S(1)}, u32[]{:S(2)}, u32[]{:S(2)}) collective-permute-start(bf16[1,16,128]{2,1,0:T(8,128)(2,1)S(1)} %get-tuple-element.55), channel_id=1, source_target_pairs={{0,8},{8,16},{16,24},{1,9},{9,17},{17,25},{2,10},{10,18},{18,26},{... | collective-permute-start | bytes 12296 | tf_op jit(solution)/shard_map/ppermute | solution.py:20
  180.3 7.5 %collective-permute-start.13 = (bf16[1,16,128]{2,1,0:T(8,128)(2,1)S(1)}, bf16[1,16,128]{2,1,0:T(8,128)(2,1)S(1)}, u32[]{:S(2)}, u32[]{:S(2)}) collective-permute-start(bf16[1,16,128]{2,1,0:T(8,128)(2,1)S(1)} %get-tuple-element.56), channel_id=1, source_target_pairs={{8,0},{16,8},{24,16},{9,1},{17,9},{25,17},{10,2},{18,10},{26,18},{... | collective-permute-start | bytes 12296 | tf_op jit(solution)/shard_map/ppermute | solution.py:22
  182.8 1.1 copy-start.6
  184.5 11.0 %copy-start.16 = (bf16[3,3,128,128]{3,2,1,0:T(8,128)(2,1)S(1)}, bf16[3,3,128,128]{3,2,1,0:T(8,128)(2,1)}, u32[]{:S(2)}) copy-start(bf16[3,3,128,128]{3,2,1,0:T(8,128)(2,1)} %param.10) | copy-start | bytes 884740
  185.0 4.1 %copy-start.18 = (f32[9,128,128]{2,1,0:T(8,128)}, f32[9,128,128]{2,1,0:T(8,128)S(1)}, u32[]{:S(2)}) copy-start(f32[9,128,128]{2,1,0:T(8,128)S(1)} %fusion.21) | copy-start | bytes 1769476
  185.1 60.2 %collective-permute-start.6 = (bf16[34,1,256]{2,1,0:T(2,128)(2,1)S(1)}, bf16[34,1,256]{2,1,0:T(2,128)(2,1)S(1)}, u32[]{:S(2)}, u32[]{:S(2)}) collective-permute-start(bf16[34,1,256]{2,1,0:T(2,128)(2,1)S(1)} %get-tuple-element.65), channel_id=1, source_target_pairs={{0,1},{1,2},{2,3},{3,4},{4,5},{5,6},{6,7},{8,9},{9,10},{10,11},{11... | collective-permute-start | bytes 52232 | tf_op jit(solution)/shard_map/ppermute | solution.py:20
  186.4 58.9 %collective-permute-start.7 = (bf16[34,1,256]{2,1,0:T(2,128)(2,1)S(1)}, bf16[34,1,256]{2,1,0:T(2,128)(2,1)S(1)}, u32[]{:S(2)}, u32[]{:S(2)}) collective-permute-start(bf16[34,1,256]{2,1,0:T(2,128)(2,1)S(1)} %get-tuple-element.66), channel_id=1, source_target_pairs={{1,0},{2,1},{3,2},{4,3},{5,4},{6,5},{7,6},{9,8},{10,9},{11,10},{12... | collective-permute-start | bytes 52232 | tf_op jit(solution)/shard_map/ppermute | solution.py:22
  187.8 8.8 %collective-permute-start.14 = (bf16[66,1,128]{2,1,0:T(2,128)(2,1)S(1)}, bf16[66,1,128]{2,1,0:T(2,128)(2,1)S(1)}, u32[]{:S(2)}, u32[]{:S(2)}) collective-permute-start(bf16[66,1,128]{2,1,0:T(2,128)(2,1)S(1)} %get-tuple-element.45), channel_id=1, source_target_pairs={{1,0},{2,1},{3,2},{4,3},{5,4},{6,5},{7,6},{9,8},{10,9},{11,10},{12... | collective-permute-start | bytes 50696 | tf_op jit(solution)/shard_map/ppermute | solution.py:22
  189.1 7.5 %collective-permute-start.15 = (bf16[66,1,128]{2,1,0:T(2,128)(2,1)S(1)}, bf16[66,1,128]{2,1,0:T(2,128)(2,1)S(1)}, u32[]{:S(2)}, u32[]{:S(2)}) collective-permute-start(bf16[66,1,128]{2,1,0:T(2,128)(2,1)S(1)} %get-tuple-element.46), channel_id=1, source_target_pairs={{0,1},{1,2},{2,3},{3,4},{4,5},{5,6},{6,7},{8,9},{9,10},{10,11},{11... | collective-permute-start | bytes 50696 | tf_op jit(solution)/shard_map/ppermute | solution.py:20
  198.8 0.7 copy-start.22
  198.8 0.7 copy-start.23
  245.5 1.0 copy-start.17
  248.5 1.4 copy-start.4
  250.5 1.0 copy-start.13
  390.4 2.0 copy-start.20
Sparse Core Ops, SparseCore 0:
  250.1 140.2 all-reduce.6
where the time goes:
time: 404 us; the launch traced here: 403 us
  blocking collectives  168 us (42%)
  waiting for transfers between devices  139 us (34%)
  starting transfers between devices  39.2 us (10%)
  matrix products  19.7 us (5%)
  between operations  15.1 us (4%)
  local copies, waits for them, and re-layouts  15 us (4%)
  other arithmetic  6.97 us (2%)
    psum x4, blocking collectives, global_sums(): return lax.psum((pair[0], pair[1]), ('gy', 'gx'))  168 us
    psum x1, waiting for transfers between devices, on_device(): lax.psum((fine_weight_grad, fine_gain_grad, projection_grad, coarse_weigh...  138 us
    ppermute x8, starting transfers between devices, extended(): lax.ppermute(tail, axis, [(i, (i + 1) % count) for i in range(ends)])  28.8 us
    unnamed x55, local copies, waits for them, and re-layouts  11.6 us
    ppermute x8, starting transfers between devices, extended(): lax.ppermute(head, axis, [((i + 1) % count, i) for i in range(ends)])  10.3 us
  transfers between devices with their start and end apart: 17, of which 2 were waited for; matrix products, arithmetic and copies ran while one was open for 5% of the time, Pallas kernels for 0%

commit v1 on v0

v1 whole, which is shorter than its diff:
```python
import functools

import jax
import jax.numpy as jnp
from jax import lax
from jax.experimental import pallas as pl
from jax.experimental.pallas import tpu as pltpu
from jax.sharding import PartitionSpec as P

GROUPS = 32
EPSILON = 1e-05
F32 = jnp.float32
BF16 = jnp.bfloat16
MESH = pl.DeviceIdType.MESH
DIRS = ((1, 0), (-1, 0), (0, 1), (0, -1), (1, 1), (1, -1), (-1, 1), (-1, -1))


def round_up(value, unit):
    return -(-value // unit) * unit


def log2(value):
    assert value & (value - 1) == 0
    return value.bit_length() - 1


def cell_of(shape, pitch):
    index = lax.broadcasted_iota(jnp.int32, shape, 0)
    return lax.shift_right_logical(index, log2(pitch)), index & (pitch - 1)


def within(value, low, high):
    return (value >= low) & (value < high)


def group_sums(sums, per_group):
    channels = sums.shape[1]
    bits = log2(per_group)
    one = lax.broadcasted_iota(jnp.int32, (channels, channels), 0)
    two = lax.broadcasted_iota(jnp.int32, (channels, channels), 1)
    same = lax.shift_right_logical(one, bits) == lax.shift_right_logical(two, bits)
    padded = jnp.concatenate([sums, jnp.zeros((8 - sums.shape[0], channels), F32)], axis=0)
    total = jnp.dot(
        padded, same.astype(F32), precision=lax.Precision.HIGHEST, preferred_element_type=F32
    )
    return total


def matmul_nt(left, right):
    return lax.dot_general(left, right, (((1,), (1,)), ((), ())), preferred_element_type=F32)


def matmul_tn(left, right):
    return lax.dot_general(left, right, (((0,), (0,)), ((), ())), preferred_element_type=F32)


def split_rows(sums):
    return jnp.concatenate([sums[:, :128], sums[:, 128:]], axis=0)


class Reducer:
    def __init__(self, levels, rows, data, full, landings, sends, recvs):
        self.levels, self.rows = levels, rows
        self.data, self.full, self.landings = data, full, landings
        self.sends, self.recvs = sends, recvs

    def span(self, base, count):
        return pl.ds(pl.multiple_of(base, 16), count)

    def offset(self, depth):
        base, size = 0, self.rows
        for _, count, index, _ in self.levels[:depth]:
            size //= count
            base = base + index * size
        return base, size

    def copies(self, stage):
        depth = len(self.levels)
        gather = stage >= depth
        level = 2 * depth - 1 - stage if gather else stage
        _, count, index, device = self.levels[level]
        base, size = self.offset(level)
        part = size // count
        out = []
        for step in range(1, count):
            peer = lax.rem(index + step, count)
            if gather:
                own = self.full.at[self.span(base + index * part, part)]
                src, dst, theirs = own, own, self.full.at[self.span(base + peer * part, part)]
            else:
                src = self.data.at[self.span(base + peer * part, part)]
                dst = self.landings[level].at[index]
                theirs = self.landings[level].at[peer]
            out.append((
                pltpu.make_async_remote_copy(
                    src_ref=src, dst_ref=dst,
                    send_sem=self.sends.at[stage, step], recv_sem=self.recvs.at[stage, index],
                    device_id=device(peer), device_id_type=MESH,
                ),
                pltpu.make_async_remote_copy(
                    src_ref=theirs, dst_ref=theirs,
                    send_sem=self.sends.at[stage, step], recv_sem=self.recvs.at[stage, peer],
                    device_id=device(peer), device_id_type=MESH,
                ),
            ))
        return out

    def start(self, stage):
        for copy, _ in self.copies(stage):
            copy.start()

    def finish(self, stage):
        depth = len(self.levels)
        for copy, arrival in self.copies(stage):
            copy.wait_send()
            arrival.wait_recv()
        if stage < depth:
            _, count, index, _ = self.levels[stage]
            base, size = self.offset(stage)
            part = size // count
            mine = self.span(base + index * part, part)
            landing = self.landings[stage]
            landing[index] = self.data[mine]
            total = landing[0].astype(F32)
            for source in range(1, count):
                total = total + landing[source].astype(F32)
            target = self.full if stage == depth - 1 else self.data
            target[mine] = total.astype(BF16)


def kernel(sizes, field, cot, gain_f, wf, proj, gain_c, wc,
           cout, fgrad, wf_grad, gf_grad, proj_grad, wc_grad, gc_grad,
           E, HF, X3f, PU, CI, HC, X3c, C, X3g, DC, D, X3d, T,
           row_out, col_out, row_in, col_in, slots,
           data_c, full_c, lc1, lc2, lc3, data_f, full_f, lf1, lf2, lf3,
           rim_send, rim_recv, sum_send, sum_recv, c_send, c_recv, f_send, f_recv):
    H, W, h, w, wp, wpc, ngy, ngx = sizes
    c1, c2 = proj.shape
    count_all = ngy * ngx
    gy, gx = lax.axis_index("gy"), lax.axis_index("gx")
    me = gy * ngx + gx
    fine_count = float(H * W * count_all * (c1 // GROUPS))
    coarse_count = float(h * w * count_all * (c2 // GROUPS))

    def peer_of(step):
        peer = lax.rem(me + step, count_all)
        return peer, (lax.div(peer, ngx), lax.rem(peer, ngx))

    barrier = pltpu.get_barrier_semaphore()

    @pl.loop(1, count_all)
    def _(step):
        pl.semaphore_signal(barrier, inc=1, device_id=peer_of(step)[1], device_id_type=MESH)

    def sum_copy(turn, step):
        peer, device = peer_of(step)
        go = pltpu.make_async_remote_copy(
            src_ref=slots.at[turn, me], dst_ref=slots.at[turn, me],
            send_sem=sum_send.at[step], recv_sem=sum_recv.at[turn % 2, me],
            device_id=device, device_id_type=MESH)
        come = pltpu.make_async_remote_copy(
            src_ref=slots.at[turn, peer], dst_ref=slots.at[turn, peer],
            send_sem=sum_send.at[step], recv_sem=sum_recv.at[turn % 2, peer],
            device_id=device, device_id_type=MESH)
        return go, come

    def sums_start(turn, rows):
        pad = jnp.zeros((8 - rows.shape[0], 128), F32)
        slots[turn, me] = jnp.concatenate([rows, pad], axis=0)

        @pl.loop(1, count_all)
        def _(step):
            sum_copy(turn, step)[0].start()

    def sums_finish(turn):
        @pl.loop(1, count_all)
        def _(step):
            go, come = sum_copy(turn, step)
            go.wait_send()
            come.wait_recv()
        return jnp.sum(slots[turn], axis=0)

    values = field[...].astype(F32)
    sums_f = jnp.concatenate([
        jnp.sum(values, axis=(0, 1), keepdims=True).reshape(1, c1),
        jnp.sum(values * values, axis=(0, 1), keepdims=True).reshape(1, c1)], axis=0)
    E[...] = jnp.zeros(E.shape, F32)
    E[pl.ds(3 * wp + 3, H * wp), :] = jnp.concatenate(
        [values, jnp.zeros((H, wp - W, c1), F32)], axis=1).reshape(H * wp, c1)
    grads = jnp.concatenate([cot[...].astype(F32), jnp.zeros((h, wpc - w, c2), F32)], axis=1)
    grads = grads.reshape(h * wpc, c2)
    C[...] = jnp.zeros(C.shape, F32)
    for half in range(2):
        C[half, pl.ds(2 * wpc + 2, h * wpc), :] = grads[:, half * 128:(half + 1) * 128]

    fr, cr = 3 * wp, 2 * wpc
    for side, (first, first_c) in enumerate(((H, h), (3, 2))):
        row_out[side, 0:fr] = E[first * wp:first * wp + fr].astype(BF16)
        for half in range(2):
            row_out[side, fr + half * cr:fr + (half + 1) * cr] = (
                C[half, first_c * wpc:first_c * wpc + cr].astype(BF16))
    for side, (first, first_c) in enumerate(((W, w), (3, 2))):
        for col in range(3):
            col_out[side, col * H:(col + 1) * H] = (
                E[pl.ds(3 * wp + first + col, H, stride=wp), :].astype(BF16))
        for half in range(2):
            for col in range(2):
                at = 3 * H + (2 * half + col) * h
                col_out[side, at:at + h] = (
                    C[half, pl.ds(2 * wpc + first_c + col, h, stride=wpc), :].astype(BF16))

    pl.semaphore_wait(barrier, count_all - 1)
    sums_start(0, sums_f)

    def rim_copy(number):
        dy, dx = DIRS[number]
        if dy != 0:
            src = row_out.at[0 if dy > 0 else 1]
            dst = row_in.at[number]
        else:
            src = col_out.at[0 if dx > 0 else 1]
            dst = col_in.at[number - 2]
        return pltpu.make_async_remote_copy(
            src_ref=src, dst_ref=dst, send_sem=rim_send.at[number], recv_sem=rim_recv.at[number],
            device_id=(gy + dy, gx + dx), device_id_type=MESH)

    def reaches(dy, dx):
        return within(gy + dy, 0, ngy) & within(gx + dx, 0, ngx)

    for number, (dy, dx) in enumerate(DIRS):
        @pl.when(reaches(dy, dx))
        def _():
            rim_copy(number).start()

    _, col_f = cell_of((fr, 128), wp)
    _, col_c = cell_of((cr, 128), wpc)

    def place(piece, dx, width, rim, cols):
        if dx == 0:
            return piece
        gap = jnp.zeros((width, 128), F32)
        if dx > 0:
            return jnp.where(cols < rim, jnp.concatenate([piece[width:], gap], axis=0), 0.0)
        moved = jnp.concatenate([gap, piece[:piece.shape[0] - width]], axis=0)
        return jnp.where(within(cols, width + rim, width + 2 * rim), moved, 0.0)

    for number, (dy, dx) in enumerate(DIRS):
        @pl.when(reaches(-dy, -dx))
        def _():
            rim_copy(number).wait_recv()
            if dy != 0:
                at = 0 if dy > 0 else (H + 3) * wp
                piece = row_in[number, 0:fr].astype(F32)
                E[at:at + fr] = E[at:at + fr] + place(piece, dx, W, 3, col_f)
                at = 0 if dy > 0 else (h + 2) * wpc
                for half in range(2):
                    piece = row_in[number, fr + half * cr:fr + (half + 1) * cr].astype(F32)
                    C[half, at:at + cr] = C[half, at:at + cr] + place(piece, dx, w, 2, col_c)
            else:
                at = 0 if dx > 0 else W + 3
                for col in range(3):
                    E[pl.ds(3 * wp + at + col, H, stride=wp), :] = (
                        col_in[number - 2, col * H:(col + 1) * H].astype(F32))
                at = 0 if dx > 0 else w + 2
                for half in range(2):
                    for col in range(2):
                        row = 3 * H + (2 * half + col) * h
                        C[half, pl.ds(2 * wpc + at + col, h, stride=wpc), :] = (
                            col_in[number - 2, row:row + h].astype(F32))

    ext = (h + 2) * wpc
    for tap in range(3):
        for half in range(2):
            at = tap * c2 + half * 128
            X3g[:, at:at + 128] = C[half, pl.ds(tap, (h + 4) * wpc), :].astype(BF16)
    raw = jnp.zeros((ext, c2), F32)
    for a in range(3):
        for b in range(3):
            raw = raw + matmul_nt(X3g[a * wpc:a * wpc + ext, b * c2:(b + 1) * c2],
                                  wc[2 - a, (2 - b) * c2:(3 - b) * c2, :])
    DC[...] = raw

    total = group_sums(sums_finish(0)[0:2], c1 // GROUPS)
    avg_f = total[0:1] / fine_count
    inv_f = lax.rsqrt(total[1:2] / fine_count - avg_f * avg_f + EPSILON)
    gain = gain_f[...]
    row, col = cell_of(E.shape, wp)
    inside = (within(row + (gy * H - 3), 0, H * ngy) & within(col + (gx * W - 3), 0, W * ngx))
    act = (E[...] - avg_f) * inv_f * gain
    HF[...] = jnp.where(inside, act / (1.0 + jnp.exp(-act)), 0.0)
    for tap in range(3):
        X3f[:, tap * c1:(tap + 1) * c1] = HF[pl.ds(tap, (H + 6) * wp), :].astype(BF16)
    span = (H + 4) * wp
    block = E[pl.ds(wp + 1, span), :]
    for a in range(3):
        block = block + jnp.dot(X3f[a * wp:a * wp + span, :], wf[a], preferred_element_type=F32)
    block = block.astype(BF16).astype(F32).reshape(h + 2, 2, wp, c1)
    PU[...] = (block[:, 0] + block[:, 1]).reshape((h + 2) * wp, c1)
    pooled = ((PU[pl.ds(0, ext, stride=2), :] + PU[pl.ds(1, ext, stride=2), :]) * 0.25)
    prow, pcol = cell_of((ext, c1), wpc)
    inner_p = within(prow, 1, h + 1) & within(pcol, 1, w + 1)
    pooled_in = jnp.where(inner_p, pooled, 0.0).astype(BF16)
    coarse_in = jnp.dot(pooled.astype(BF16), proj[...], preferred_element_type=F32)
    coarse_in = coarse_in.astype(BF16).astype(F32)
    CI[...] = coarse_in
    prow, pcol = cell_of((ext, c2), wpc)
    inner = within(prow, 1, h + 1) & within(pcol, 1, w + 1)
    kept = jnp.where(inner, coarse_in, 0.0)
    sums_start(1, split_rows(jnp.concatenate([
        jnp.sum(kept, axis=0, keepdims=True), jnp.sum(kept * kept, axis=0, keepdims=True)], axis=0)))

    def joined(rows):
        return jnp.concatenate([rows[0:2], rows[2:4]], axis=1)

    total = group_sums(joined(sums_finish(1)), c2 // GROUPS)
    avg_c = total[0:1] / coarse_count
    inv_c = lax.rsqrt(total[1:2] / coarse_count - avg_c * avg_c + EPSILON)
    gain2 = gain_c[...]
    inside_c = (within(prow + (gy * h - 1), 0, h * ngy) & within(pcol + (gx * w - 1), 0, w * ngx))
    norm_c = (CI[...] - avg_c) * inv_c
    act = norm_c * gain2
    sigma = 1.0 / (1.0 + jnp.exp(-act))
    dact_c = DC[...] * (sigma * (1.0 + act * (1.0 - sigma)))
    DC[...] = dact_c
    kept = jnp.where(inner, dact_c, 0.0)
    sums_start(2, split_rows(jnp.concatenate([
        jnp.sum(kept, axis=0, keepdims=True),
        jnp.sum(kept * norm_c, axis=0, keepdims=True)], axis=0)))

    HC[0:ext] = jnp.where(inside_c, act * sigma, 0.0)
    HC[ext:] = jnp.zeros((HC.shape[0] - ext, c2), F32)
    for tap in range(3):
        X3c[:, tap * c2:(tap + 1) * c2] = HC[pl.ds(tap, ext), :].astype(BF16)
    cells_c = h * wpc
    gb = grads.astype(BF16)
    taps_c = 3 * c2
    for a in range(3):
        part = matmul_tn(X3c[a * wpc:a * wpc + cells_c, :], gb).astype(BF16)
        for half in range(2):
            at = (3 * half + a) * taps_c
            data_c[at:at + taps_c] = part[:, half * 128:(half + 1) * 128]
    if data_c.shape[0] > 6 * taps_c:
        data_c[6 * taps_c:] = jnp.zeros((data_c.shape[0] - 6 * taps_c, 128), BF16)

    core, chip = lax.rem(gx, 2), lax.div(gx, 2)
    levels = (
        ("core", 2, core, lambda k: (gy, chip * 2 + k)),
        ("chip", ngx // 2, chip, lambda k: (gy, k * 2 + core)),
        ("gy", ngy, gy, lambda k: (k, gx)),
    )
    big = Reducer(levels, data_c.shape[0], data_c, full_c, (lc1, lc2, lc3), c_send, c_recv)
    small = Reducer(levels, data_f.shape[0], data_f, full_f, (lf1, lf2, lf3), f_send, f_recv)
    big.start(0)

    out = CI[pl.ds(wpc + 1, cells_c), :]
    for a in range(3):
        out = out + jnp.dot(X3c[a * wpc:a * wpc + cells_c, :], wc[a], preferred_element_type=F32)
    cout[...] = out.reshape(h, wpc, c2)[:, :w].astype(BF16)

    big.finish(0)
    big.start(1)

    total = joined(sums_finish(2))
    gc_grad[...] = total[1:2]
    total = group_sums(total[0:2] * gain2, c2 // GROUPS)
    first, second = total[0:1] / coarse_count, total[1:2] / coarse_count
    norm_c = (CI[...] - avg_c) * inv_c
    dcoarse = inv_c * (DC[...] * gain2 - first - norm_c * second)
    dcoarse = dcoarse + jnp.concatenate(
        [C[0, pl.ds(wpc + 1, ext), :], C[1, pl.ds(wpc + 1, ext), :]], axis=1)
    dcoarse = jnp.where(inside_c, dcoarse, 0.0).astype(BF16)
    pgrad = matmul_tn(pooled_in, dcoarse).astype(BF16)
    taps_f = 9 * c1
    for half in range(2):
        at = taps_f + half * c1
        data_f[at:at + c1] = pgrad[:, half * 128:(half + 1) * 128]
    if data_f.shape[0] > taps_f + 2 * c1:
        data_f[taps_f + 2 * c1:] = jnp.zeros((data_f.shape[0] - taps_f - 2 * c1, 128), BF16)
    dsmall = (matmul_nt(dcoarse, proj[...]) * 0.25).astype(BF16).astype(F32)
    PU[pl.ds(0, ext, stride=2), :] = dsmall
    PU[pl.ds(1, ext, stride=2), :] = dsmall
    wide = PU[...].reshape(h + 2, 1, wp, c1)
    D[0:span] = jnp.broadcast_to(wide, (h + 2, 2, wp, c1)).reshape(span, c1)
    D[span:] = jnp.zeros((D.shape[0] - span, c1), F32)
    for tap in range(3):
        X3d[:, tap * c1:(tap + 1) * c1] = D[pl.ds(tap, span), :].astype(BF16)
    cells_f = H * wp
    dact = jnp.zeros((cells_f, c1), F32)
    for a in range(3):
        for b in range(3):
            dact = dact + matmul_nt(X3d[(1 + a) * wp:(1 + a) * wp + cells_f, b * c1:(b + 1) * c1],
                                    wf[2 - a, (2 - b) * c1:(3 - b) * c1, :])
    norm_f = (E[pl.ds(3 * wp + 2, cells_f), :] - avg_f) * inv_f
    act = norm_f * gain
    sigma = 1.0 / (1.0 + jnp.exp(-act))
    dact = dact * (sigma * (1.0 + act * (1.0 - sigma)))
    _, col = cell_of((cells_f, c1), wp)
    kept = jnp.where(within(col, 1, W + 1), dact, 0.0)
    sums_start(3, jnp.concatenate([
        jnp.sum(kept, axis=0, keepdims=True),
        jnp.sum(kept * norm_f, axis=0, keepdims=True)], axis=0))
    T[0:cells_f] = dact

    big.finish(1)
    big.start(2)

    gm = jnp.where(within(col, 2, W + 2), D[2 * wp:2 * wp + cells_f], 0.0).astype(BF16)
    for a in range(3):
        part = matmul_tn(X3f[(2 + a) * wp:(2 + a) * wp + cells_f, :], gm)
        data_f[a * 3 * c1:(a + 1) * 3 * c1] = part.astype(BF16)
    small.start(0)
    big.finish(2)
    big.start(3)
    small.finish(0)
    small.start(1)

    total = sums_finish(3)[0:2]
    gf_grad[...] = total[1:2]
    total = group_sums(total * gain, c1 // GROUPS)
    first, second = total[0:1] / fine_count, total[1:2] / fine_count
    norm_f = (E[pl.ds(3 * wp + 2, cells_f), :] - avg_f) * inv_f
    result = inv_f * (T[0:cells_f] * gain - first - norm_f * second)
    T[0:cells_f] = result + D[pl.ds(2 * wp + 1, cells_f), :]
    T[cells_f:] = jnp.zeros((T.shape[0] - cells_f, c1), F32)
    fgrad[...] = T[pl.ds(1, cells_f), :].reshape(H, wp, c1)[:, :W].astype(BF16)

    big.finish(3)
    big.start(4)
    small.finish(1)
    small.start(2)
    small.finish(2)
    small.start(3)
    big.finish(4)
    big.start(5)
    small.finish(3)
    small.start(4)
    small.finish(4)
    small.start(5)
    big.finish(5)
    for half in range(2):
        at = 3 * half * taps_c
        wc_grad[:, half * 128:(half + 1) * 128] = full_c[at:at + 3 * taps_c].astype(F32)
    small.finish(5)
    wf_grad[...] = full_f[0:taps_f].astype(F32)
    for half in range(2):
        at = taps_f + half * c1
        proj_grad[:, half * 128:(half + 1) * 128] = full_f[at:at + c1].astype(F32)

    for number, (dy, dx) in enumerate(DIRS):
        @pl.when(reaches(dy, dx))
        def _():
            rim_copy(number).wait_send()


def on_device(field, cotangent, gain_fine, weight_fine, projection, gain_coarse, weight_coarse):
    H, W, c1 = field.shape
    h, w, c2 = cotangent.shape
    ngy, ngx = lax.axis_size("gy"), lax.axis_size("gx")
    everyone = ngy * ngx
    wpc = round_up(w + 4, 16)
    wp = 2 * wpc
    sizes = (H, W, h, w, wp, wpc, ngy, ngx)
    rows_c = everyone * round_up(-(-18 * c2 // everyone), 16)
    rows_f = everyone * round_up(-(-11 * c1 // everyone), 16)
    counts = (2, ngx // 2, ngy)
    most = max(counts)

    def landings(rows):
        out = []
        for count in counts:
            rows //= count
            out.append(pltpu.VMEM((count, rows, 128), BF16))
        return out

    DMA = pltpu.SemaphoreType.DMA
    scratch = [
        pltpu.VMEM(((H + 8) * wp, c1), F32),
        pltpu.VMEM(((H + 8) * wp, c1), F32),
        pltpu.VMEM(((H + 6) * wp, 3 * c1), BF16),
        pltpu.VMEM(((h + 2) * wp, c1), F32),
        pltpu.VMEM(((h + 2) * wpc, c2), F32),
        pltpu.VMEM(((h + 4) * wpc, c2), F32),
        pltpu.VMEM(((h + 2) * wpc, 3 * c2), BF16),
        pltpu.VMEM((2, (h + 6) * wpc, 128), F32),
        pltpu.VMEM(((h + 4) * wpc, 3 * c2), BF16),
        pltpu.VMEM(((h + 2) * wpc, c2), F32),
        pltpu.VMEM(((H + 6) * wp, c1), F32),
        pltpu.VMEM(((H + 4) * wp, 3 * c1), BF16),
        pltpu.VMEM(((H + 1) * wp, c1), F32),
        pltpu.VMEM((2, 3 * wp + 4 * wpc, 128), BF16),
        pltpu.VMEM((2, 3 * H + 4 * h, 128), BF16),
        pltpu.VMEM((8, 3 * wp + 4 * wpc, 128), BF16),
        pltpu.VMEM((2, 3 * H + 4 * h, 128), BF16),
        pltpu.VMEM((4, everyone, 8, 128), F32),
        pltpu.VMEM((rows_c, 128), BF16), pltpu.VMEM((rows_c, 128), BF16), *landings(rows_c),
        pltpu.VMEM((rows_f, 128), BF16), pltpu.VMEM((rows_f, 128), BF16), *landings(rows_f),
        DMA((8,)), DMA((8,)),
        DMA((everyone,)), DMA((2, everyone)),
        DMA((6, most)), DMA((6, most)),
        DMA((6, most)), DMA((6, most)),
    ]
    vmem = pl.BlockSpec(memory_space=pltpu.VMEM)
    shapes = (
        jax.ShapeDtypeStruct((h, w, c2), BF16),
        jax.ShapeDtypeStruct((H, W, c1), BF16),
        jax.ShapeDtypeStruct((9 * c1, c1), F32),
        jax.ShapeDtypeStruct((1, c1), F32),
        jax.ShapeDtypeStruct((c1, c2), F32),
        jax.ShapeDtypeStruct((9 * c2, c2), F32),
        jax.ShapeDtypeStruct((1, c2), F32),
    )
    cout, fgrad, wf_grad, gf_grad, proj_grad, wc_grad, gc_grad = pl.pallas_call(
        functools.partial(kernel, sizes),
        out_shape=shapes,
        in_specs=[vmem] * 7,
        out_specs=[vmem] * 7,
        scratch_shapes=scratch,
        compiler_params=pltpu.CompilerParams(
            collective_id=0, has_side_effects=True, vmem_limit_bytes=52 * 2**20),
    )(
        field, cotangent, gain_fine.reshape(1, c1), weight_fine.reshape(3, 3 * c1, c1),
        projection, gain_coarse.reshape(1, c2), weight_coarse.reshape(3, 3 * c2, c2),
    )
    return (
        cout, fgrad, wf_grad.reshape(3, 3, c1, c1), gf_grad.reshape(c1), proj_grad,
        wc_grad.reshape(3, 3, c2, c2), gc_grad.reshape(c2),
    )


def solution(mesh):
    return jax.shard_map(
        on_device,
        mesh=mesh,
        in_specs=(P("gy", "gx", None), P("gy", "gx", None), P(), P(), P(), P(), P()),
        out_specs=(P("gy", "gx", None), P("gy", "gx", None), P(), P(), P(), P(), P()),
        check_vma=False,
    )
```

time: 404 us -> 77.3 us (0.19)
  blocking collectives: 168 us -> 0 us
  waiting for transfers between devices: 139 us -> 0 us
  Pallas kernels: 0 us -> 64.2 us
  starting transfers between devices: 39.2 us -> 0 us
  matrix products: 19.7 us -> 0 us
  between operations: 15.1 us -> 0.66 us
  other arithmetic: 6.97 us -> 0 us
    psum x4 -> x0, blocking collectives: 168 us -> none  [global_sums(): return lax.psum((pair[0], pair[1]), ('gy', 'gx'))]
    psum x1 -> x0, waiting for transfers between devices: 138 us -> none  [on_device(): lax.psum((fine_weight_grad, fine_gain_grad, projection_grad, coarse_weigh...]
    pallas_call x0 -> x1, Pallas kernels: none -> 64.2 us  [on_device(): pl.pallas_call(functools.partial(kernel, sizes), out_shape=shapes, in_spe...]
    ppermute x16 -> x0, starting transfers between devices: 39.2 us -> none  [the longest x8 28.8 us: extended(): lax.ppermute(tail, axis, [(i, (i + 1) % count) for i in range(ends)])]
    dot_general x57 -> x0, matrix products: 19.7 us -> none  [the longest x18 7.19 us: conv_transpose(): jnp.dot(window, weight[row_tap, col_tap].T, preferred_element_type=jnp.fl...]
    unnamed x55 -> x19, local copies, waits for them, and re-layouts: 11.6 us -> 12.1 us
  transfers between devices with their start and end apart: 17 -> 0, of which waited for: 2 -> 0; matrix products, arithmetic and copies ran while one was open for 5% -> 0% of each run, Pallas kernels for 0% -> 0%
where the time goes in v1:
time: 77.3 us; the launch traced here: 77 us
  Pallas kernels  64.2 us (83%)
  local copies, waits for them, and re-layouts  12.1 us (16%)
    pallas_call x1, Pallas kernels, on_device(): pl.pallas_call(functools.partial(kernel, sizes), out_shape=shapes, in_spe...  64.2 us
    unnamed x19, local copies, waits for them, and re-layouts  12.1 us

profile of v1, /device:TPU:0, one launch (start us, length us, event | category | flops | bytes accessed | tf_op | source)
XLA Modules:
  0.0 77.0 jit_solution(5677172440470634632)
XLA Ops:
  0.6 0.0 copy-start
  0.6 1.0 %copy-done = bf16[3,3,128,128]{3,2,1,0:T(8,128)(2,1)S(1)} copy-done((bf16[3,3,128,128]{3,2,1,0:T(8,128)(2,1)S(1)}, bf16[3,3,128,128]{3,2,1,0:T(8,128)(2,1)}, u32[]{:S(2)}) %copy-start) | copy-done | bytes 294936
  1.6 0.0 copy-start.1
  1.6 0.9 %copy-done.1 = bf16[64,16,128]{2,1,0:T(8,128)(2,1)S(1)} copy-done((bf16[64,16,128]{2,1,0:T(8,128)(2,1)S(1)}, bf16[64,16,128]{2,1,0:T(8,128)(2,1)}, u32[]{:S(2)}) %copy-start.1) | copy-done | bytes 262168
  2.5 0.0 copy-start.2
  2.5 0.9 %copy-done.2 = bf16[32,8,256]{2,1,0:T(8,128)(2,1)S(1)} copy-done((bf16[32,8,256]{2,1,0:T(8,128)(2,1)S(1)}, bf16[32,8,256]{2,1,0:T(8,128)(2,1)}, u32[]{:S(2)}) %copy-start.2) | copy-done | bytes 131096
  3.5 0.0 copy-start.3
  3.5 0.8 %copy-done.3 = bf16[128,256]{1,0:T(8,128)(2,1)S(1)} copy-done((bf16[128,256]{1,0:T(8,128)(2,1)S(1)}, bf16[128,256]{1,0:T(8,128)(2,1)}, u32[]{:S(2)}) %copy-start.3) | copy-done | bytes 65560
  4.3 0.0 copy-start.4
  4.3 0.7 copy-done.4
  5.0 0.0 copy-start.5
  5.0 0.7 copy-done.5
  5.6 64.2 %shard_map.126 = (bf16[32,8,256]{2,1,0:T(8,128)(2,1)S(1)}, bf16[64,16,128]{2,1,0:T(8,128)(2,1)S(1)}, f32[1152,128]{1,0:T(8,128)S(1)}, f32[1,128]{1,0:T(1,128)S(1...) custom-call(bf16[64,16,128]{2,1,0:T(8,128)(2,1)S(1)} %copy-done.1, ...), custom_call_target="tpu_custom_call" | custom-call | tf_op jit(solution)/shard_map/pallas_call | solution.py:512
  69.9 0.7 copy.21
  70.5 0.7 copy.22
  71.2 0.8 %copy.23 = f32[3,3,128,128]{3,2,1,0:T(8,128)} copy(f32[3,3,128,128]{3,2,1,0:T(8,128)S(1)} %bitcast.8) | data formatting | bytes 1179648
  72.1 0.5 copy.24
  72.6 0.7 copy.25
  73.2 3.2 %copy.26 = f32[3,3,256,256]{3,2,1,0:T(8,128)} copy(f32[3,3,256,256]{3,2,1,0:T(8,128)} %bitcast.14) | data formatting | bytes 4718592
  76.4 0.6 copy.27
Async XLA Ops:
  0.6 1.0 %copy-start = (bf16[3,3,128,128]{3,2,1,0:T(8,128)(2,1)S(1)}, bf16[3,3,128,128]{3,2,1,0:T(8,128)(2,1)}, u32[]{:S(2)}) copy-start(bf16[3,3,128,128]{3,2,1,0:T(8,128)(2,1)} %param.10) | copy-start | bytes 884740
  1.6 0.9 %copy-start.1 = (bf16[64,16,128]{2,1,0:T(8,128)(2,1)S(1)}, bf16[64,16,128]{2,1,0:T(8,128)(2,1)}, u32[]{:S(2)}) copy-start(bf16[64,16,128]{2,1,0:T(8,128)(2,1)} %field.1) | copy-start | bytes 786436
  2.5 0.9 %copy-start.2 = (bf16[32,8,256]{2,1,0:T(8,128)(2,1)S(1)}, bf16[32,8,256]{2,1,0:T(8,128)(2,1)}, u32[]{:S(2)}) copy-start(bf16[32,8,256]{2,1,0:T(8,128)(2,1)} %cot.1) | copy-start | bytes 393220
  3.5 0.8 %copy-start.3 = (bf16[128,256]{1,0:T(8,128)(2,1)S(1)}, bf16[128,256]{1,0:T(8,128)(2,1)}, u32[]{:S(2)}) copy-start(bf16[128,256]{1,0:T(8,128)(2,1)} %proj.1) | copy-start | bytes 196612
  4.3 0.7 copy-start.4
  5.0 0.7 copy-start.5

commit v2 on v1

--- a/solution.py
+++ b/solution.py
@@ -128,8 +128,10 @@
             target[mine] = total.astype(BF16)
 
 
-def kernel(sizes, field, cot, gain_f, wf, proj, gain_c, wc,
-           cout, fgrad, wf_grad, gf_grad, proj_grad, wc_grad, gc_grad,
+def kernel(sizes, field_h, cot_h, gain_f_h, wf_h, proj_h, gain_c_h, wc_h,
+           cout_h, fgrad_h, wf_grad_h, gf_grad_h, proj_grad_h, wc_grad_h, gc_grad_h,
+           cout, fgrad, wf_grad, gf_grad, proj_grad, wc_grad, gc_grad, store_sem,
+           field, cot, gain_f, wf, proj, gain_c, wc, load_sem,
            E, HF, X3f, PU, CI, HC, X3c, C, X3g, DC, D, X3d, T,
            row_out, col_out, row_in, col_in, slots,
            data_c, full_c, lc1, lc2, lc3, data_f, full_f, lf1, lf2, lf3,
@@ -142,15 +144,48 @@
     fine_count = float(H * W * count_all * (c1 // GROUPS))
     coarse_count = float(h * w * count_all * (c2 // GROUPS))
 
+    def wrapped(place, count):
+        return jnp.where(place >= count, place - count, place)
+
+    few = count_all <= 64
+    if few:
+        rows_of = [wrapped(gy + dy, ngy) for dy in range(ngy)]
+        cols_of = [wrapped(gx + dx, ngx) for dx in range(ngx)]
+
     def peer_of(step):
+        if few:
+            place = (rows_of[step // ngx], cols_of[step % ngx])
+            return place[0] * ngx + place[1], place
         peer = lax.rem(me + step, count_all)
         return peer, (lax.div(peer, ngx), lax.rem(peer, ngx))
 
+    def each_peer(body):
+        if few:
+            for step in range(1, count_all):
+                body(step)
+        else:
+            pl.loop(1, count_all)(body)
+
+    loads = [
+        pltpu.make_async_copy(src, dst, load_sem.at[number])
+        for number, (src, dst) in enumerate(zip(
+            (field_h, cot_h, gain_f_h, wf_h, proj_h, gain_c_h, wc_h),
+            (field, cot, gain_f, wf, proj, gain_c, wc)))
+    ]
+    for number in (0, 1, 6, 2, 3, 4, 5):
+        loads[number].start()
+    stores = [
+        pltpu.make_async_copy(src, dst, store_sem.at[number])
+        for number, (src, dst) in enumerate(zip(
+            (cout, fgrad, wf_grad, gf_grad, proj_grad, wc_grad, gc_grad),
+            (cout_h, fgrad_h, wf_grad_h, gf_grad_h, proj_grad_h, wc_grad_h, gc_grad_h)))
+    ]
     barrier = pltpu.get_barrier_semaphore()
 
-    @pl.loop(1, count_all)
-    def _(step):
+    def greet(step):
         pl.semaphore_signal(barrier, inc=1, device_id=peer_of(step)[1], device_id_type=MESH)
+
+    each_peer(greet)
 
     def sum_copy(turn, step):
         peer, device = peer_of(step)
@@ -168,18 +203,18 @@
         pad = jnp.zeros((8 - rows.shape[0], 128), F32)
         slots[turn, me] = jnp.concatenate([rows, pad], axis=0)
 
-        @pl.loop(1, count_all)
-        def _(step):
-            sum_copy(turn, step)[0].start()
+        each_peer(lambda step: sum_copy(turn, step)[0].start())
 
     def sums_finish(turn):
-        @pl.loop(1, count_all)
-        def _(step):
+        def settle(step):
             go, come = sum_copy(turn, step)
             go.wait_send()
             come.wait_recv()
+
+        each_peer(settle)
         return jnp.sum(slots[turn], axis=0)
 
+    loads[0].wait()
     values = field[...].astype(F32)
     sums_f = jnp.concatenate([
         jnp.sum(values, axis=(0, 1), keepdims=True).reshape(1, c1),
@@ -187,6 +222,7 @@
     E[...] = jnp.zeros(E.shape, F32)
     E[pl.ds(3 * wp + 3, H * wp), :] = jnp.concatenate(
         [values, jnp.zeros((H, wp - W, c1), F32)], axis=1).reshape(H * wp, c1)
+    loads[1].wait()
     grads = jnp.concatenate([cot[...].astype(F32), jnp.zeros((h, wpc - w, c2), F32)], axis=1)
     grads = grads.reshape(h * wpc, c2)
     C[...] = jnp.zeros(C.shape, F32)
@@ -273,6 +309,7 @@
         for half in range(2):
             at = tap * c2 + half * 128
             X3g[:, at:at + 128] = C[half, pl.ds(tap, (h + 4) * wpc), :].astype(BF16)
+    loads[6].wait()
     raw = jnp.zeros((ext, c2), F32)
     for a in range(3):
         for b in range(3):
@@ -280,6 +317,8 @@
                                   wc[2 - a, (2 - b) * c2:(3 - b) * c2, :])
     DC[...] = raw
 
+    for number in (2, 3, 4, 5):
+        loads[number].wait()
     total = group_sums(sums_finish(0)[0:2], c1 // GROUPS)
     avg_f = total[0:1] / fine_count
     inv_f = lax.rsqrt(total[1:2] / fine_count - avg_f * avg_f + EPSILON)
@@ -332,10 +371,11 @@
     for tap in range(3):
         X3c[:, tap * c2:(tap + 1) * c2] = HC[pl.ds(tap, ext), :].astype(BF16)
     cells_c = h * wpc
-    gb = grads.astype(BF16)
+    gb = grads.T.astype(BF16)
     taps_c = 3 * c2
     for a in range(3):
-        part = matmul_tn(X3c[a * wpc:a * wpc + cells_c, :], gb).astype(BF16)
+        part = jnp.dot(gb, X3c[a * wpc:a * wpc + cells_c, :], preferred_element_type=F32)
+        part = part.T.astype(BF16)
         for half in range(2):
             at = (3 * half + a) * taps_c
             data_c[at:at + taps_c] = part[:, half * 128:(half + 1) * 128]
@@ -356,12 +396,14 @@
     for a in range(3):
         out = out + jnp.dot(X3c[a * wpc:a * wpc + cells_c, :], wc[a], preferred_element_type=F32)
     cout[...] = out.reshape(h, wpc, c2)[:, :w].astype(BF16)
+    stores[0].start()
 
     big.finish(0)
     big.start(1)
 
     total = joined(sums_finish(2))
     gc_grad[...] = total[1:2]
+    stores[6].start()
     total = group_sums(total[0:2] * gain2, c2 // GROUPS)
     first, second = total[0:1] / coarse_count, total[1:2] / coarse_count
     norm_c = (CI[...] - avg_c) * inv_c
@@ -382,9 +424,17 @@
     wide = PU[...].reshape(h + 2, 1, wp, c1)
     D[0:span] = jnp.broadcast_to(wide, (h + 2, 2, wp, c1)).reshape(span, c1)
     D[span:] = jnp.zeros((D.shape[0] - span, c1), F32)
+    cells_f = H * wp
+    _, col = cell_of((cells_f, c1), wp)
+    gm = jnp.where(within(col, 2, W + 2), D[2 * wp:2 * wp + cells_f], 0.0).T.astype(BF16)
+    for a in range(3):
+        part = jnp.dot(gm, X3f[(2 + a) * wp:(2 + a) * wp + cells_f, :], preferred_element_type=F32)
+        data_f[a * 3 * c1:(a + 1) * 3 * c1] = part.T.astype(BF16)
+    small.start(0)
+    big.finish(1)
+    big.start(2)
     for tap in range(3):
         X3d[:, tap * c1:(tap + 1) * c1] = D[pl.ds(tap, span), :].astype(BF16)
-    cells_f = H * wp
     dact = jnp.zeros((cells_f, c1), F32)
     for a in range(3):
         for b in range(3):
@@ -394,28 +444,24 @@
     act = norm_f * gain
     sigma = 1.0 / (1.0 + jnp.exp(-act))
     dact = dact * (sigma * (1.0 + act * (1.0 - sigma)))
-    _, col = cell_of((cells_f, c1), wp)
     kept = jnp.where(within(col, 1, W + 1), dact, 0.0)
     sums_start(3, jnp.concatenate([
         jnp.sum(kept, axis=0, keepdims=True),
         jnp.sum(kept * norm_f, axis=0, keepdims=True)], axis=0))
     T[0:cells_f] = dact
 
-    big.finish(1)
-    big.start(2)
-
-    gm = jnp.where(within(col, 2, W + 2), D[2 * wp:2 * wp + cells_f], 0.0).astype(BF16)
-    for a in range(3):
-        part = matmul_tn(X3f[(2 + a) * wp:(2 + a) * wp + cells_f, :], gm)
-        data_f[a * 3 * c1:(a + 1) * 3 * c1] = part.astype(BF16)
-    small.start(0)
+    small.finish(0)
+    small.start(1)
     big.finish(2)
     big.start(3)
-    small.finish(0)
-    small.start(1)
 
     total = sums_finish(3)[0:2]
+    big.finish(3)
+    big.start(4)
+    small.finish(1)
+    small.start(2)
     gf_grad[...] = total[1:2]
+    stores[3].start()
     total = group_sums(total * gain, c1 // GROUPS)
     first, second = total[0:1] / fine_count, total[1:2] / fine_count
     norm_f = (E[pl.ds(3 * wp + 2, cells_f), :] - avg_f) * inv_f
@@ -423,33 +469,54 @@
     T[0:cells_f] = result + D[pl.ds(2 * wp + 1, cells_f), :]
     T[cells_f:] = jnp.zeros((T.shape[0] - cells_f, c1), F32)
     fgrad[...] = T[pl.ds(1, cells_f), :].reshape(H, wp, c1)[:, :W].astype(BF16)
-
-    big.finish(3)
-    big.start(4)
-    small.finish(1)
-    small.start(2)
+    stores[1].start()
+
     small.finish(2)
     small.start(3)
+    small.finish(3)
+    small.start(4)
     big.finish(4)
     big.start(5)
-    small.finish(3)
-    small.start(4)
     small.finish(4)
     small.start(5)
     big.finish(5)
     for half in range(2):
         at = 3 * half * taps_c
-        wc_grad[:, half * 128:(half + 1) * 128] = full_c[at:at + 3 * taps_c].astype(F32)
+        wc_grad[:, half * 128:(half + 1) * 128] = full_c[at:at + 3 * taps_c]
+    stores[5].start()
     small.finish(5)
-    wf_grad[...] = full_f[0:taps_f].astype(F32)
+    wf_grad[...] = full_f[0:taps_f]
+    stores[2].start()
     for half in range(2):
         at = taps_f + half * c1
-        proj_grad[:, half * 128:(half + 1) * 128] = full_f[at:at + c1].astype(F32)
+        proj_grad[:, half * 128:(half + 1) * 128] = full_f[at:at + c1]
+    stores[4].start()
+    for copy in stores:
+        copy.wait()
 
     for number, (dy, dx) in enumerate(DIRS):
         @pl.when(reaches(dy, dx))
         def _():
             rim_copy(number).wait_send()
+
+
+def deliver(cout, fgrad, wf_grad, gf_grad, proj_grad, wc_grad, gc_grad, *rest):
+    outs, held, wide, load_sem, store_sem = rest[:7], rest[7:14], rest[14:17], rest[17], rest[18]
+    sources = (cout, fgrad, wf_grad, gf_grad, proj_grad, wc_grad, gc_grad)
+    ready = list(held)
+    ready[5], ready[2], ready[4] = wide
+    order = (5, 2, 4, 1, 0, 3, 6)
+    loads = [pltpu.make_async_copy(sources[k], held[k], load_sem.at[k]) for k in range(7)]
+    stores = [pltpu.make_async_copy(ready[k], outs[k], store_sem.at[k]) for k in range(7)]
+    for k in order:
+        loads[k].start()
+    for k in order:
+        loads[k].wait()
+        if ready[k] is not held[k]:
+            ready[k][...] = held[k][...].astype(F32)
+        stores[k].start()
+    for k in order:
+        stores[k].wait()
 
 
 def on_device(field, cotangent, gain_fine, weight_fine, projection, gain_coarse, weight_coarse):
@@ -474,6 +541,14 @@
 
     DMA = pltpu.SemaphoreType.DMA
     scratch = [
+        pltpu.VMEM((H, W, c1), BF16),
+        pltpu.VMEM((h, w, c2), BF16),
+        pltpu.VMEM((1, c1), F32),
+        pltpu.VMEM((3, 3 * c1, c1), BF16),
+        pltpu.VMEM((c1, c2), BF16),
+        pltpu.VMEM((1, c2), F32),
+        pltpu.VMEM((3, 3 * c2, c2), BF16),
+        DMA((7,)),
         pltpu.VMEM(((H + 8) * wp, c1), F32),
         pltpu.VMEM(((H + 8) * wp, c1), F32),
         pltpu.VMEM(((H + 6) * wp, 3 * c1), BF16),
@@ -499,28 +574,42 @@
         DMA((6, most)), DMA((6, most)),
         DMA((6, most)), DMA((6, most)),
     ]
-    vmem = pl.BlockSpec(memory_space=pltpu.VMEM)
-    shapes = (
-        jax.ShapeDtypeStruct((h, w, c2), BF16),
-        jax.ShapeDtypeStruct((H, W, c1), BF16),
-        jax.ShapeDtypeStruct((9 * c1, c1), F32),
-        jax.ShapeDtypeStruct((1, c1), F32),
-        jax.ShapeDtypeStruct((c1, c2), F32),
-        jax.ShapeDtypeStruct((9 * c2, c2), F32),
-        jax.ShapeDtypeStruct((1, c2), F32),
-    )
-    cout, fgrad, wf_grad, gf_grad, proj_grad, wc_grad, gc_grad = pl.pallas_call(
+    def shapes(kind):
+        return (
+            jax.ShapeDtypeStruct((h, w, c2), BF16),
+            jax.ShapeDtypeStruct((H, W, c1), BF16),
+            jax.ShapeDtypeStruct((9 * c1, c1), kind),
+            jax.ShapeDtypeStruct((1, c1), F32),
+            jax.ShapeDtypeStruct((c1, c2), kind),
+            jax.ShapeDtypeStruct((9 * c2, c2), kind),
+            jax.ShapeDtypeStruct((1, c2), F32),
+        )
+
+    hbm = pl.BlockSpec(memory_space=pltpu.HBM)
+    results = pl.pallas_call(
         functools.partial(kernel, sizes),
-        out_shape=shapes,
-        in_specs=[vmem] * 7,
-        out_specs=[vmem] * 7,
-        scratch_shapes=scratch,
+        out_shape=shapes(BF16),
+        in_specs=[hbm] * 7,
+        out_specs=[hbm] * 7,
+        scratch_shapes=[pltpu.VMEM(shape.shape, shape.dtype) for shape in shapes(BF16)]
+        + [DMA((7,))] + scratch,
         compiler_params=pltpu.CompilerParams(
-            collective_id=0, has_side_effects=True, vmem_limit_bytes=52 * 2**20),
+            collective_id=0, has_side_effects=True, vmem_limit_bytes=63 * 2**20),
     )(
         field, cotangent, gain_fine.reshape(1, c1), weight_fine.reshape(3, 3 * c1, c1),
         projection, gain_coarse.reshape(1, c2), weight_coarse.reshape(3, 3 * c2, c2),
     )
+    cout, fgrad, wf_grad, gf_grad, proj_grad, wc_grad, gc_grad = pl.pallas_call(
+        deliver,
+        out_shape=shapes(F32),
+        in_specs=[hbm] * 7,
+        out_specs=[hbm] * 7,
+        scratch_shapes=[pltpu.VMEM(shape.shape, shape.dtype) for shape in shapes(BF16)] + [
+            pltpu.VMEM((9 * c2, c2), F32), pltpu.VMEM((9 * c1, c1), F32),
+            pltpu.VMEM((c1, c2), F32), DMA((7,)), DMA((7,)),
+        ],
+        compiler_params=pltpu.CompilerParams(vmem_limit_bytes=63 * 2**20),
+    )(*results)
     return (
         cout, fgrad, wf_grad.reshape(3, 3, c1, c1), gf_grad.reshape(c1), proj_grad,
         wc_grad.reshape(3, 3, c2, c2), gc_grad.reshape(c2),

time: 77.3 us -> 66.6 us (0.86)
  local copies, waits for them, and re-layouts: 12.1 us -> 0 us
  Pallas kernels: 64.2 us -> 65.8 us
    unnamed x19 -> x0, local copies, waits for them, and re-layouts: 12.1 us -> none
    pallas_call x1 -> x2, Pallas kernels: 64.2 us -> 65.8 us  [the longest x1 62.5 us: on_device(): pl.pallas_call(functools.partial(kernel, sizes), out_shape=shapes(BF16),...]
where the time goes in v2:
time: 66.6 us; the launch traced here: 66.4 us
  Pallas kernels  65.8 us (99%)
    pallas_call x1, Pallas kernels, on_device(): pl.pallas_call(functools.partial(kernel, sizes), out_shape=shapes(BF16),...  62.5 us
    pallas_call x1, Pallas kernels, on_device(): pl.pallas_call(deliver, out_shape=shapes(F32), in_specs=[hbm] * 7, out_sp...  3.31 us

profile of v2, /device:TPU:0, one launch (start us, length us, event | category | flops | bytes accessed | tf_op | source)
XLA Modules:
  0.0 66.4 jit_solution(8077596125822650104)
XLA Ops:
  0.6 62.5 %shard_map.126 = (bf16[32,8,256]{2,1,0:T(8,128)(2,1)}, bf16[64,16,128]{2,1,0:T(8,128)(2,1)}, bf16[1152,128]{1,0:T(8,128)(2,1)}, f32[1,128]{1,0:T(1,128)}, bf16[1...) custom-call(bf16[64,16,128]{2,1,0:T(8,128)(2,1)} %field_h.1, bf16[32,8,256]{2,1,0:T(8,128)(2,1)} %cot_h.1, ...), custom_call_target="tpu_custom_call" | custom-call | tf_op jit(solution)/shard_map/pallas_call | solution.py:589
  63.1 3.3 %shard_map.127 = (bf16[32,8,256]{2,1,0:T(8,128)(2,1)}, bf16[64,16,128]{2,1,0:T(8,128)(2,1)}, f32[1152,128]{1,0:T(8,128)}, f32[1,128]{1,0:T(1,128)}, f32[128,256]...) custom-call(bf16[32,8,256]{2,1,0:T(8,128)(2,1)} %get-tuple-element.21.cout, ...), custom_call_target="tpu_custom_call" | custom-call | tf_op jit(solution)/shard_map/pallas_call | solution.py:602

commit v3 on v2

--- a/solution.py
+++ b/solution.py
@@ -39,11 +39,28 @@
     one = lax.broadcasted_iota(jnp.int32, (channels, channels), 0)
     two = lax.broadcasted_iota(jnp.int32, (channels, channels), 1)
     same = lax.shift_right_logical(one, bits) == lax.shift_right_logical(two, bits)
-    padded = jnp.concatenate([sums, jnp.zeros((8 - sums.shape[0], channels), F32)], axis=0)
-    total = jnp.dot(
-        padded, same.astype(F32), precision=lax.Precision.HIGHEST, preferred_element_type=F32
-    )
-    return total
+    high = sums.astype(BF16)
+    rest = sums - high.astype(F32)
+    middle = rest.astype(BF16)
+    low = (rest - middle.astype(F32)).astype(BF16)
+    count = sums.shape[0]
+    pad = jnp.zeros((16 - 3 * count, channels), F32)
+    parts = jnp.concatenate(
+        [high.astype(F32), middle.astype(F32), low.astype(F32), pad], axis=0).astype(BF16)
+    total = jnp.dot(parts, same.astype(F32).astype(BF16), preferred_element_type=F32)
+    return total[0:count] + total[count:2 * count] + total[2 * count:3 * count]
+
+
+def sigmoid(act):
+    return 0.5 + 0.5 * jnp.tanh(0.5 * act)
+
+
+def fold(values):
+    return jnp.sum(values.reshape(-1, 8, values.shape[1]), axis=0)
+
+
+def unfold(partial):
+    return jnp.sum(partial, axis=0, keepdims=True)
 
 
 def matmul_nt(left, right):
@@ -128,14 +145,27 @@
             target[mine] = total.astype(BF16)
 
 
+class Pair:
+    def __init__(self, *members):
+        self.members = members
+
+    def start(self, stage):
+        for member in self.members:
+            member.start(stage)
+
+    def finish(self, stage):
+        for member in self.members:
+            member.finish(stage)
+
+
 def kernel(sizes, field_h, cot_h, gain_f_h, wf_h, proj_h, gain_c_h, wc_h,
            cout_h, fgrad_h, wf_grad_h, gf_grad_h, proj_grad_h, wc_grad_h, gc_grad_h,
            cout, fgrad, wf_grad, gf_grad, proj_grad, wc_grad, gc_grad, store_sem,
            field, cot, gain_f, wf, proj, gain_c, wc, load_sem,
            E, HF, X3f, PU, CI, HC, X3c, C, X3g, DC, D, X3d, T,
            row_out, col_out, row_in, col_in, slots,
-           data_c, full_c, lc1, lc2, lc3, data_f, full_f, lf1, lf2, lf3,
-           rim_send, rim_recv, sum_send, sum_recv, c_send, c_recv, f_send, f_recv):
+           data_c, full_c, lc1, lc2, lc3, data_b, full_b, lb1, lb2, lb3, data_f, full_f, lf1, lf2, lf3,
+           rim_send, rim_recv, sum_send, sum_recv, c_send, c_recv, b_send, b_recv, f_send, f_recv):
     H, W, h, w, wp, wpc, ngy, ngx = sizes
     c1, c2 = proj.shape
     count_all = ngy * ngx
@@ -308,14 +338,14 @@
     for tap in range(3):
         for half in range(2):
             at = tap * c2 + half * 128
-            X3g[:, at:at + 128] = C[half, pl.ds(tap, (h + 4) * wpc), :].astype(BF16)
+            for go in range(0, (h + 4) * wpc, 4 * wpc):
+                X3g[go:go + 4 * wpc, at:at + 128] = (
+                    C[half, pl.ds(tap + go, 4 * wpc), :].astype(BF16))
     loads[6].wait()
-    raw = jnp.zeros((ext, c2), F32)
-    for a in range(3):
-        for b in range(3):
-            raw = raw + matmul_nt(X3g[a * wpc:a * wpc + ext, b * c2:(b + 1) * c2],
-                                  wc[2 - a, (2 - b) * c2:(3 - b) * c2, :])
-    DC[...] = raw
+    cells = jnp.concatenate([X3g[a * wpc:a * wpc + ext, :] for a in range(3)], axis=1)
+    taps = jnp.concatenate(
+        [wc[2 - a, (2 - b) * c2:(3 - b) * c2, :] for a in range(3) for b in range(3)], axis=1)
+    DC[...] = matmul_nt(cells, taps)
 
     for number in (2, 3, 4, 5):
         loads[number].wait()
@@ -323,18 +353,25 @@
     avg_f = total[0:1] / fine_count
     inv_f = lax.rsqrt(total[1:2] / fine_count - avg_f * avg_f + EPSILON)
     gain = gain_f[...]
-    row, col = cell_of(E.shape, wp)
-    inside = (within(row + (gy * H - 3), 0, H * ngy) & within(col + (gx * W - 3), 0, W * ngx))
-    act = (E[...] - avg_f) * inv_f * gain
-    HF[...] = jnp.where(inside, act / (1.0 + jnp.exp(-act)), 0.0)
+    scale_f = inv_f * gain
+    shift_f = -avg_f * scale_f
+    row, col = cell_of((4 * wp, c1), wp)
+    col_inside = within(col + (gx * W - 3), 0, W * ngx)
+    for go in range(0, (H + 8) * wp, 4 * wp):
+        act = E[go:go + 4 * wp] * scale_f + shift_f
+        inside = col_inside & within(row + (gy * H - 3 + go // wp), 0, H * ngy)
+        HF[go:go + 4 * wp] = jnp.where(inside, act * sigmoid(act), 0.0)
     for tap in range(3):
-        X3f[:, tap * c1:(tap + 1) * c1] = HF[pl.ds(tap, (H + 6) * wp), :].astype(BF16)
+        for go in range(0, (H + 6) * wp, 2 * wp):
+            X3f[go:go + 2 * wp, tap * c1:(tap + 1) * c1] = (
+                HF[pl.ds(tap + go, 2 * wp), :].astype(BF16))
     span = (H + 4) * wp
-    block = E[pl.ds(wp + 1, span), :]
-    for a in range(3):
-        block = block + jnp.dot(X3f[a * wp:a * wp + span, :], wf[a], preferred_element_type=F32)
-    block = block.astype(BF16).astype(F32).reshape(h + 2, 2, wp, c1)
-    PU[...] = (block[:, 0] + block[:, 1]).reshape((h + 2) * wp, c1)
+    cells = jnp.concatenate([X3f[a * wp:a * wp + span, :] for a in range(3)], axis=1)
+    HF[0:span] = jnp.dot(cells, wf[...].reshape(9 * c1, c1), preferred_element_type=F32)
+    for go in range(0, span, 4 * wp):
+        block = HF[go:go + 4 * wp] + E[pl.ds(wp + 1 + go, 4 * wp), :]
+        block = block.astype(BF16).astype(F32).reshape(2, 2, wp, c1)
+        PU[go // 2:go // 2 + 2 * wp] = (block[:, 0] + block[:, 1]).reshape(2 * wp, c1)
     pooled = ((PU[pl.ds(0, ext, stride=2), :] + PU[pl.ds(1, ext, stride=2), :]) * 0.25)
     prow, pcol = cell_of((ext, c1), wpc)
     inner_p = within(prow, 1, h + 1) & within(pcol, 1, w + 1)
@@ -342,11 +379,22 @@
     coarse_in = jnp.dot(pooled.astype(BF16), proj[...], preferred_element_type=F32)
     coarse_in = coarse_in.astype(BF16).astype(F32)
     CI[...] = coarse_in
-    prow, pcol = cell_of((ext, c2), wpc)
-    inner = within(prow, 1, h + 1) & within(pcol, 1, w + 1)
-    kept = jnp.where(inner, coarse_in, 0.0)
-    sums_start(1, split_rows(jnp.concatenate([
-        jnp.sum(kept, axis=0, keepdims=True), jnp.sum(kept * kept, axis=0, keepdims=True)], axis=0)))
+    step_c = 2 * wpc
+    prow, pcol = cell_of((step_c, c2), wpc)
+    pcol_inner = within(pcol, 1, w + 1)
+    pcol_inside = within(pcol + (gx * w - 1), 0, w * ngx)
+
+    def inner_at(go):
+        return pcol_inner & within(prow + go // wpc, 1, h + 1)
+
+    def inside_at(go):
+        return pcol_inside & within(prow + (gy * h - 1 + go // wpc), 0, h * ngy)
+
+    one, two = jnp.zeros((8, c2), F32), jnp.zeros((8, c2), F32)
+    for go in range(0, ext, step_c):
+        kept = jnp.where(inner_at(go), CI[go:go + step_c], 0.0)
+        one, two = one + fold(kept), two + fold(kept * kept)
+    sums_start(1, split_rows(jnp.concatenate([unfold(one), unfold(two)], axis=0)))
 
     def joined(rows):
         return jnp.concatenate([rows[0:2], rows[2:4]], axis=1)
@@ -355,32 +403,35 @@
     avg_c = total[0:1] / coarse_count
     inv_c = lax.rsqrt(total[1:2] / coarse_count - avg_c * avg_c + EPSILON)
     gain2 = gain_c[...]
-    inside_c = (within(prow + (gy * h - 1), 0, h * ngy) & within(pcol + (gx * w - 1), 0, w * ngx))
-    norm_c = (CI[...] - avg_c) * inv_c
-    act = norm_c * gain2
-    sigma = 1.0 / (1.0 + jnp.exp(-act))
-    dact_c = DC[...] * (sigma * (1.0 + act * (1.0 - sigma)))
-    DC[...] = dact_c
-    kept = jnp.where(inner, dact_c, 0.0)
-    sums_start(2, split_rows(jnp.concatenate([
-        jnp.sum(kept, axis=0, keepdims=True),
-        jnp.sum(kept * norm_c, axis=0, keepdims=True)], axis=0)))
-
-    HC[0:ext] = jnp.where(inside_c, act * sigma, 0.0)
+    one, two = jnp.zeros((8, c2), F32), jnp.zeros((8, c2), F32)
+    for go in range(0, ext, step_c):
+        norm_c = (CI[go:go + step_c] - avg_c) * inv_c
+        act = norm_c * gain2
+        sigma = sigmoid(act)
+        dact_c = DC[go:go + step_c] * (sigma * (1.0 + act * (1.0 - sigma)))
+        DC[go:go + step_c] = dact_c
+        kept = jnp.where(inner_at(go), dact_c, 0.0)
+        one, two = one + fold(kept), two + fold(kept * norm_c)
+        HC[go:go + step_c] = jnp.where(inside_at(go), act * sigma, 0.0)
+    sums_start(2, split_rows(jnp.concatenate([unfold(one), unfold(two)], axis=0)))
     HC[ext:] = jnp.zeros((HC.shape[0] - ext, c2), F32)
     for tap in range(3):
-        X3c[:, tap * c2:(tap + 1) * c2] = HC[pl.ds(tap, ext), :].astype(BF16)
+        for go in range(0, ext, step_c):
+            X3c[go:go + step_c, tap * c2:(tap + 1) * c2] = (
+                HC[pl.ds(tap + go, step_c), :].astype(BF16))
     cells_c = h * wpc
     gb = grads.T.astype(BF16)
     taps_c = 3 * c2
     for a in range(3):
         part = jnp.dot(gb, X3c[a * wpc:a * wpc + cells_c, :], preferred_element_type=F32)
         part = part.T.astype(BF16)
+        target, base = (data_c, a * 2 * taps_c) if a < 2 else (data_b, 0)
         for half in range(2):
-            at = (3 * half + a) * taps_c
-            data_c[at:at + taps_c] = part[:, half * 128:(half + 1) * 128]
-    if data_c.shape[0] > 6 * taps_c:
-        data_c[6 * taps_c:] = jnp.zeros((data_c.shape[0] - 6 * taps_c, 128), BF16)
+            at = base + half * taps_c
+            target[at:at + taps_c] = part[:, half * 128:(half + 1) * 128]
+    for target, used in ((data_c, 4 * taps_c), (data_b, 2 * taps_c)):
+        if target.shape[0] > used:
+            target[used:] = jnp.zeros((target.shape[0] - used, 128), BF16)
 
     core, chip = lax.rem(gx, 2), lax.div(gx, 2)
     levels = (
@@ -388,14 +439,18 @@
         ("chip", ngx // 2, chip, lambda k: (gy, k * 2 + core)),
         ("gy", ngy, gy, lambda k: (k, gx)),
     )
-    big = Reducer(levels, data_c.shape[0], data_c, full_c, (lc1, lc2, lc3), c_send, c_recv)
+    turned = (levels[0], levels[2], levels[1])
+    big = Pair(
+        Reducer(levels, data_c.shape[0], data_c, full_c, (lc1, lc2, lc3), c_send, c_recv),
+        Reducer(turned, data_b.shape[0], data_b, full_b, (lb1, lb2, lb3), b_send, b_recv))
     small = Reducer(levels, data_f.shape[0], data_f, full_f, (lf1, lf2, lf3), f_send, f_recv)
     big.start(0)
 
-    out = CI[pl.ds(wpc + 1, cells_c), :]
-    for a in range(3):
-        out = out + jnp.dot(X3c[a * wpc:a * wpc + cells_c, :], wc[a], preferred_element_type=F32)
-    cout[...] = out.reshape(h, wpc, c2)[:, :w].astype(BF16)
+    cells = jnp.concatenate([X3c[a * wpc:a * wpc + cells_c, :] for a in range(3)], axis=1)
+    HC[0:cells_c] = jnp.dot(cells, wc[...].reshape(9 * c2, c2), preferred_element_type=F32)
+    for go in range(0, cells_c, step_c):
+        out = HC[go:go + step_c] + CI[pl.ds(wpc + 1 + go, step_c), :]
+        cout[go // wpc:go // wpc + 2] = out.reshape(2, wpc, c2)[:, :w].astype(BF16)
     stores[0].start()
 
     big.finish(0)
@@ -406,11 +461,14 @@
     stores[6].start()
     total = group_sums(total[0:2] * gain2, c2 // GROUPS)
     first, second = total[0:1] / coarse_count, total[1:2] / coarse_count
-    norm_c = (CI[...] - avg_c) * inv_c
-    dcoarse = inv_c * (DC[...] * gain2 - first - norm_c * second)
-    dcoarse = dcoarse + jnp.concatenate(
-        [C[0, pl.ds(wpc + 1, ext), :], C[1, pl.ds(wpc + 1, ext), :]], axis=1)
-    dcoarse = jnp.where(inside_c, dcoarse, 0.0).astype(BF16)
+    scale_c = inv_c * gain2
+    for go in range(0, ext, step_c):
+        norm_c = (CI[go:go + step_c] - avg_c) * inv_c
+        dcoarse = DC[go:go + step_c] * scale_c - inv_c * (first + norm_c * second)
+        dcoarse = dcoarse + jnp.concatenate(
+            [C[half, pl.ds(wpc + 1 + go, step_c), :] for half in range(2)], axis=1)
+        X3g[go:go + step_c, 0:c2] = jnp.where(inside_at(go), dcoarse, 0.0).astype(BF16)
+    dcoarse = X3g[0:ext, 0:c2]
     pgrad = matmul_tn(pooled_in, dcoarse).astype(BF16)
     taps_f = 9 * c1
     for half in range(2):
@@ -421,8 +479,10 @@
     dsmall = (matmul_nt(dcoarse, proj[...]) * 0.25).astype(BF16).astype(F32)
     PU[pl.ds(0, ext, stride=2), :] = dsmall
     PU[pl.ds(1, ext, stride=2), :] = dsmall
-    wide = PU[...].reshape(h + 2, 1, wp, c1)
-    D[0:span] = jnp.broadcast_to(wide, (h + 2, 2, wp, c1)).reshape(span, c1)
+    for pair in range(h + 2):
+        wide = PU[pair * wp:(pair + 1) * wp]
+        D[2 * pair * wp:(2 * pair + 1) * wp] = wide
+        D[(2 * pair + 1) * wp:(2 * pair + 2) * wp] = wide
     D[span:] = jnp.zeros((D.shape[0] - span, c1), F32)
     cells_f = H * wp
     _, col = cell_of((cells_f, c1), wp)
@@ -434,21 +494,26 @@
     big.finish(1)
     big.start(2)
     for tap in range(3):
-        X3d[:, tap * c1:(tap + 1) * c1] = D[pl.ds(tap, span), :].astype(BF16)
-    dact = jnp.zeros((cells_f, c1), F32)
-    for a in range(3):
-        for b in range(3):
-            dact = dact + matmul_nt(X3d[(1 + a) * wp:(1 + a) * wp + cells_f, b * c1:(b + 1) * c1],
-                                    wf[2 - a, (2 - b) * c1:(3 - b) * c1, :])
-    norm_f = (E[pl.ds(3 * wp + 2, cells_f), :] - avg_f) * inv_f
-    act = norm_f * gain
-    sigma = 1.0 / (1.0 + jnp.exp(-act))
-    dact = dact * (sigma * (1.0 + act * (1.0 - sigma)))
-    kept = jnp.where(within(col, 1, W + 1), dact, 0.0)
-    sums_start(3, jnp.concatenate([
-        jnp.sum(kept, axis=0, keepdims=True),
-        jnp.sum(kept * norm_f, axis=0, keepdims=True)], axis=0))
-    T[0:cells_f] = dact
+        for go in range(0, span, 4 * wp):
+            X3d[go:go + 4 * wp, tap * c1:(tap + 1) * c1] = (
+                D[pl.ds(tap + go, 4 * wp), :].astype(BF16))
+    cells = jnp.concatenate(
+        [X3d[(1 + a) * wp:(1 + a) * wp + cells_f, :] for a in range(3)], axis=1)
+    taps = jnp.concatenate(
+        [wf[2 - a, (2 - b) * c1:(3 - b) * c1, :] for a in range(3) for b in range(3)], axis=1)
+    T[0:cells_f] = matmul_nt(cells, taps)
+    _, col = cell_of((4 * wp, c1), wp)
+    own_col = within(col, 1, W + 1)
+    one, two = jnp.zeros((8, c1), F32), jnp.zeros((8, c1), F32)
+    for go in range(0, cells_f, 4 * wp):
+        norm_f = (E[pl.ds(3 * wp + 2 + go, 4 * wp), :] - avg_f) * inv_f
+        act = norm_f * gain
+        sigma = sigmoid(act)
+        dact = T[go:go + 4 * wp] * (sigma * (1.0 + act * (1.0 - sigma)))
+        T[go:go + 4 * wp] = dact
+        kept = jnp.where(own_col, dact, 0.0)
+        one, two = one + fold(kept), two + fold(kept * norm_f)
+    sums_start(3, jnp.concatenate([unfold(one), unfold(two)], axis=0))
 
     small.finish(0)
     small.start(1)
@@ -464,11 +529,14 @@
     stores[3].start()
     total = group_sums(total * gain, c1 // GROUPS)
     first, second = total[0:1] / fine_count, total[1:2] / fine_count
-    norm_f = (E[pl.ds(3 * wp + 2, cells_f), :] - avg_f) * inv_f
-    result = inv_f * (T[0:cells_f] * gain - first - norm_f * second)
-    T[0:cells_f] = result + D[pl.ds(2 * wp + 1, cells_f), :]
     T[cells_f:] = jnp.zeros((T.shape[0] - cells_f, c1), F32)
-    fgrad[...] = T[pl.ds(1, cells_f), :].reshape(H, wp, c1)[:, :W].astype(BF16)
+    for go in range(0, cells_f, 4 * wp):
+        norm_f = (E[pl.ds(3 * wp + 2 + go, 4 * wp), :] - avg_f) * inv_f
+        result = T[go:go + 4 * wp] * scale_f - inv_f * (first + norm_f * second)
+        T[go:go + 4 * wp] = result + D[pl.ds(2 * wp + 1 + go, 4 * wp), :]
+    for go in range(0, cells_f, 4 * wp):
+        result = T[pl.ds(1 + go, 4 * wp), :].reshape(4, wp, c1)
+        fgrad[go // wp:go // wp + 4] = result[:, :W].astype(BF16)
     stores[1].start()
 
     small.finish(2)
@@ -480,9 +548,12 @@
     small.finish(4)
     small.start(5)
     big.finish(5)
-    for half in range(2):
-        at = 3 * half * taps_c
-        wc_grad[:, half * 128:(half + 1) * 128] = full_c[at:at + 3 * taps_c]
+    for a in range(3):
+        source, base = (full_c, a * 2 * taps_c) if a < 2 else (full_b, 0)
+        for half in range(2):
+            at = base + half * taps_c
+            wc_grad[a * taps_c:(a + 1) * taps_c, half * 128:(half + 1) * 128] = (
+                source[at:at + taps_c])
     stores[5].start()
     small.finish(5)
     wf_grad[...] = full_f[0:taps_f]
@@ -527,14 +598,15 @@
     wpc = round_up(w + 4, 16)
     wp = 2 * wpc
     sizes = (H, W, h, w, wp, wpc, ngy, ngx)
-    rows_c = everyone * round_up(-(-18 * c2 // everyone), 16)
+    rows_c = everyone * round_up(-(-12 * c2 // everyone), 16)
+    rows_b = everyone * round_up(-(-6 * c2 // everyone), 16)
     rows_f = everyone * round_up(-(-11 * c1 // everyone), 16)
     counts = (2, ngx // 2, ngy)
     most = max(counts)
 
-    def landings(rows):
+    def landings(rows, order=counts):
         out = []
-        for count in counts:
+        for count in order:
             rows //= count
             out.append(pltpu.VMEM((count, rows, 128), BF16))
         return out
@@ -568,11 +640,12 @@
         pltpu.VMEM((2, 3 * H + 4 * h, 128), BF16),
         pltpu.VMEM((4, everyone, 8, 128), F32),
         pltpu.VMEM((rows_c, 128), BF16), pltpu.VMEM((rows_c, 128), BF16), *landings(rows_c),
+        pltpu.VMEM((rows_b, 128), BF16), pltpu.VMEM((rows_b, 128), BF16),
+        *landings(rows_b, (2, ngy, ngx // 2)),
         pltpu.VMEM((rows_f, 128), BF16), pltpu.VMEM((rows_f, 128), BF16), *landings(rows_f),
         DMA((8,)), DMA((8,)),
         DMA((everyone,)), DMA((2, everyone)),
-        DMA((6, most)), DMA((6, most)),
-        DMA((6, most)), DMA((6, most)),
+        *[DMA((6, most))] * 6,
     ]
     def shapes(kind):
         return (

time: 66.6 us -> 65.5 us (0.983)
  Pallas kernels: 65.8 us -> 64.7 us
    pallas_call x1, Pallas kernels: 62.5 us -> 61.4 us  [on_device(): pl.pallas_call(functools.partial(kernel, sizes), out_shape=shapes(BF16),...]
where the time goes in v3:
time: 65.5 us; the launch traced here: 65.3 us
  Pallas kernels  64.7 us (99%)
    pallas_call x1, Pallas kernels, on_device(): pl.pallas_call(functools.partial(kernel, sizes), out_shape=shapes(BF16),...  61.4 us
    pallas_call x1, Pallas kernels, on_device(): pl.pallas_call(deliver, out_shape=shapes(F32), in_specs=[hbm] * 7, out_sp...  3.31 us

profile of v3, /device:TPU:0, one launch (start us, length us, event | category | flops | bytes accessed | tf_op | source)
XLA Modules:
  0.0 65.3 jit_solution(13023707955339206072)
XLA Ops:
  0.6 61.4 %shard_map.126 = (bf16[32,8,256]{2,1,0:T(8,128)(2,1)}, bf16[64,16,128]{2,1,0:T(8,128)(2,1)}, bf16[1152,128]{1,0:T(8,128)(2,1)}, f32[1,128]{1,0:T(1,128)}, bf16[1...) custom-call(bf16[64,16,128]{2,1,0:T(8,128)(2,1)} %field_h.1, bf16[32,8,256]{2,1,0:T(8,128)(2,1)} %cot_h.1, ...), custom_call_target="tpu_custom_call" | custom-call | tf_op jit(solution)/shard_map/pallas_call | solution.py:662
  62.0 3.3 %shard_map.127 = (bf16[32,8,256]{2,1,0:T(8,128)(2,1)}, bf16[64,16,128]{2,1,0:T(8,128)(2,1)}, f32[1152,128]{1,0:T(8,128)}, f32[1,128]{1,0:T(1,128)}, f32[128,256]...) custom-call(bf16[32,8,256]{2,1,0:T(8,128)(2,1)} %get-tuple-element.21.cout, ...), custom_call_target="tpu_custom_call" | custom-call | tf_op jit(solution)/shard_map/pallas_call | solution.py:675

commit v4 on v3

--- a/solution.py
+++ b/solution.py
@@ -163,38 +163,19 @@
            cout, fgrad, wf_grad, gf_grad, proj_grad, wc_grad, gc_grad, store_sem,
            field, cot, gain_f, wf, proj, gain_c, wc, load_sem,
            E, HF, X3f, PU, CI, HC, X3c, C, X3g, DC, D, X3d, T,
-           row_out, col_out, row_in, col_in, slots,
+           row_out, col_out, row_in, col_in, gx_f, gx_c, gy_f, gy_c,
            data_c, full_c, lc1, lc2, lc3, data_b, full_b, lb1, lb2, lb3, data_f, full_f, lf1, lf2, lf3,
-           rim_send, rim_recv, sum_send, sum_recv, c_send, c_recv, b_send, b_recv, f_send, f_recv):
+           rim_send, rim_recv, sum_0, sum_1, sum_2, sum_3, c_send, c_recv, b_send, b_recv, f_send, f_recv):
     H, W, h, w, wp, wpc, ngy, ngx = sizes
+    sum_sems = (sum_0, sum_1, sum_2, sum_3)
     c1, c2 = proj.shape
     count_all = ngy * ngx
     gy, gx = lax.axis_index("gy"), lax.axis_index("gx")
-    me = gy * ngx + gx
     fine_count = float(H * W * count_all * (c1 // GROUPS))
     coarse_count = float(h * w * count_all * (c2 // GROUPS))
 
     def wrapped(place, count):
         return jnp.where(place >= count, place - count, place)
-
-    few = count_all <= 64
-    if few:
-        rows_of = [wrapped(gy + dy, ngy) for dy in range(ngy)]
-        cols_of = [wrapped(gx + dx, ngx) for dx in range(ngx)]
-
-    def peer_of(step):
-        if few:
-            place = (rows_of[step // ngx], cols_of[step % ngx])
-            return place[0] * ngx + place[1], place
-        peer = lax.rem(me + step, count_all)
-        return peer, (lax.div(peer, ngx), lax.rem(peer, ngx))
-
-    def each_peer(body):
-        if few:
-            for step in range(1, count_all):
-                body(step)
-        else:
-            pl.loop(1, count_all)(body)
 
     loads = [
         pltpu.make_async_copy(src, dst, load_sem.at[number])
@@ -212,37 +193,63 @@
     ]
     barrier = pltpu.get_barrier_semaphore()
 
-    def greet(step):
-        pl.semaphore_signal(barrier, inc=1, device_id=peer_of(step)[1], device_id_type=MESH)
-
-    each_peer(greet)
-
-    def sum_copy(turn, step):
-        peer, device = peer_of(step)
-        go = pltpu.make_async_remote_copy(
-            src_ref=slots.at[turn, me], dst_ref=slots.at[turn, me],
-            send_sem=sum_send.at[step], recv_sem=sum_recv.at[turn % 2, me],
-            device_id=device, device_id_type=MESH)
-        come = pltpu.make_async_remote_copy(
-            src_ref=slots.at[turn, peer], dst_ref=slots.at[turn, peer],
-            send_sem=sum_send.at[step], recv_sem=sum_recv.at[turn % 2, peer],
-            device_id=device, device_id_type=MESH)
-        return go, come
-
-    def sums_start(turn, rows):
-        pad = jnp.zeros((8 - rows.shape[0], 128), F32)
-        slots[turn, me] = jnp.concatenate([rows, pad], axis=0)
-
-        each_peer(lambda step: sum_copy(turn, step)[0].start())
-
-    def sums_finish(turn):
-        def settle(step):
-            go, come = sum_copy(turn, step)
+    def reaches(dy, dx):
+        return within(gy + dy, 0, ngy) & within(gx + dx, 0, ngx)
+
+    greeted = ngx - 1 + ngy - 1
+    for step in range(1, ngx):
+        pl.semaphore_signal(barrier, inc=1, device_id=(gy, wrapped(gx + step, ngx)),
+                            device_id_type=MESH)
+    for step in range(1, ngy):
+        pl.semaphore_signal(barrier, inc=1, device_id=(wrapped(gy + step, ngy), gx),
+                            device_id_type=MESH)
+    for dy, dx in DIRS[4:]:
+        there = reaches(dy, dx)
+        greeted = greeted + jnp.where(there, 1, 0)
+
+        @pl.when(there)
+        def _():
+            pl.semaphore_signal(barrier, inc=1, device_id=(gy + dy, gx + dx),
+                                device_id_type=MESH)
+
+    def sum_copies(turn, level):
+        count, index = ((ngx, gx), (ngy, gy))[level]
+        home = ((gx_f, gx_c), (gy_f, gy_c))[level][turn in (1, 2)].at[turn // 2]
+        sends, recvs = sum_sems[2 * level], sum_sems[2 * level + 1]
+        out = []
+        for step in range(1, count):
+            peer = wrapped(index + step, count)
+            device = (peer, gx) if level else (gy, peer)
+            out.append([
+                pltpu.make_async_remote_copy(
+                    src_ref=home.at[place], dst_ref=home.at[place],
+                    send_sem=sends.at[turn, step], recv_sem=recvs.at[turn, place],
+                    device_id=device, device_id_type=MESH)
+                for place in (index, peer)
+            ])
+        return home, index, out
+
+    def sums_send(turn, level, rows):
+        home, index, copies = sum_copies(turn, level)
+        home[index] = rows
+        for go, _ in copies:
+            go.start()
+
+    def sums_take(turn, level):
+        home, _, copies = sum_copies(turn, level)
+        for go, come in copies:
             go.wait_send()
             come.wait_recv()
-
-        each_peer(settle)
-        return jnp.sum(slots[turn], axis=0)
+        return jnp.sum(home[...], axis=0)
+
+    def sums_start(turn, rows):
+        sums_send(turn, 0, rows)
+
+    def sums_middle(turn):
+        sums_send(turn, 1, sums_take(turn, 0))
+
+    def sums_finish(turn):
+        return sums_take(turn, 1)
 
     loads[0].wait()
     values = field[...].astype(F32)
@@ -275,7 +282,7 @@
                 col_out[side, at:at + h] = (
                     C[half, pl.ds(2 * wpc + first_c + col, h, stride=wpc), :].astype(BF16))
 
-    pl.semaphore_wait(barrier, count_all - 1)
+    pl.semaphore_wait(barrier, greeted)
     sums_start(0, sums_f)
 
     def rim_copy(number):
@@ -289,9 +296,6 @@
         return pltpu.make_async_remote_copy(
             src_ref=src, dst_ref=dst, send_sem=rim_send.at[number], recv_sem=rim_recv.at[number],
             device_id=(gy + dy, gx + dx), device_id_type=MESH)
-
-    def reaches(dy, dx):
-        return within(gy + dy, 0, ngy) & within(gx + dx, 0, ngx)
 
     for number, (dy, dx) in enumerate(DIRS):
         @pl.when(reaches(dy, dx))
@@ -334,6 +338,8 @@
                         C[half, pl.ds(2 * wpc + at + col, h, stride=wpc), :] = (
                             col_in[number - 2, row:row + h].astype(F32))
 
+    sums_middle(0)
+
     ext = (h + 2) * wpc
     for tap in range(3):
         for half in range(2):
@@ -349,7 +355,7 @@
 
     for number in (2, 3, 4, 5):
         loads[number].wait()
-    total = group_sums(sums_finish(0)[0:2], c1 // GROUPS)
+    total = group_sums(sums_finish(0), c1 // GROUPS)
     avg_f = total[0:1] / fine_count
     inv_f = lax.rsqrt(total[1:2] / fine_count - avg_f * avg_f + EPSILON)
     gain = gain_f[...]
@@ -399,6 +405,7 @@
     def joined(rows):
         return jnp.concatenate([rows[0:2], rows[2:4]], axis=1)
 
+    sums_middle(1)
     total = group_sums(joined(sums_finish(1)), c2 // GROUPS)
     avg_c = total[0:1] / coarse_count
     inv_c = lax.rsqrt(total[1:2] / coarse_count - avg_c * avg_c + EPSILON)
@@ -419,6 +426,7 @@
         for go in range(0, ext, step_c):
             X3c[go:go + step_c, tap * c2:(tap + 1) * c2] = (
                 HC[pl.ds(tap + go, step_c), :].astype(BF16))
+    sums_middle(2)
     cells_c = h * wpc
     gb = grads.T.astype(BF16)
     taps_c = 3 * c2
@@ -517,10 +525,11 @@
 
     small.finish(0)
     small.start(1)
+    sums_middle(3)
     big.finish(2)
     big.start(3)
 
-    total = sums_finish(3)[0:2]
+    total = sums_finish(3)
     big.finish(3)
     big.start(4)
     small.finish(1)
@@ -638,13 +647,16 @@
         pltpu.VMEM((2, 3 * H + 4 * h, 128), BF16),
         pltpu.VMEM((8, 3 * wp + 4 * wpc, 128), BF16),
         pltpu.VMEM((2, 3 * H + 4 * h, 128), BF16),
-        pltpu.VMEM((4, everyone, 8, 128), F32),
+        pltpu.VMEM((2, ngx, 2, 128), F32),
+        pltpu.VMEM((2, ngx, 4, 128), F32),
+        pltpu.VMEM((2, ngy, 2, 128), F32),
+        pltpu.VMEM((2, ngy, 4, 128), F32),
         pltpu.VMEM((rows_c, 128), BF16), pltpu.VMEM((rows_c, 128), BF16), *landings(rows_c),
         pltpu.VMEM((rows_b, 128), BF16), pltpu.VMEM((rows_b, 128), BF16),
         *landings(rows_b, (2, ngy, ngx // 2)),
         pltpu.VMEM((rows_f, 128), BF16), pltpu.VMEM((rows_f, 128), BF16), *landings(rows_f),
         DMA((8,)), DMA((8,)),
-        DMA((everyone,)), DMA((2, everyone)),
+        DMA((4, ngx)), DMA((4, ngx)), DMA((4, ngy)), DMA((4, ngy)),
         *[DMA((6, most))] * 6,
     ]
     def shapes(kind):

time: 65.5 us -> 68.8 us (1.050)
  Pallas kernels: 64.7 us -> 68 us
    pallas_call x1, Pallas kernels: 61.4 us -> 64.7 us  [on_device(): pl.pallas_call(functools.partial(kernel, sizes), out_shape=shapes(BF16),...]
where the time goes in v4:
time: 68.8 us; the launch traced here: 68.6 us
  Pallas kernels  68 us (99%)
    pallas_call x1, Pallas kernels, on_device(): pl.pallas_call(functools.partial(kernel, sizes), out_shape=shapes(BF16),...  64.7 us
    pallas_call x1, Pallas kernels, on_device(): pl.pallas_call(deliver, out_shape=shapes(F32), in_specs=[hbm] * 7, out_sp...  3.31 us

profile of v4, /device:TPU:0, one launch (start us, length us, event | category | flops | bytes accessed | tf_op | source)
XLA Modules:
  0.0 68.6 jit_solution(8738110892467593803)
XLA Ops:
  0.6 64.7 %shard_map.126 = (bf16[32,8,256]{2,1,0:T(8,128)(2,1)}, bf16[64,16,128]{2,1,0:T(8,128)(2,1)}, bf16[1152,128]{1,0:T(8,128)(2,1)}, f32[1,128]{1,0:T(1,128)}, bf16[1...) custom-call(bf16[64,16,128]{2,1,0:T(8,128)(2,1)} %field_h.1, bf16[32,8,256]{2,1,0:T(8,128)(2,1)} %cot_h.1, ...), custom_call_target="tpu_custom_call" | custom-call | tf_op jit(solution)/shard_map/pallas_call | solution.py:674
  65.3 3.3 %shard_map.127 = (bf16[32,8,256]{2,1,0:T(8,128)(2,1)}, bf16[64,16,128]{2,1,0:T(8,128)(2,1)}, f32[1152,128]{1,0:T(8,128)}, f32[1,128]{1,0:T(1,128)}, f32[128,256]...) custom-call(bf16[32,8,256]{2,1,0:T(8,128)(2,1)} %get-tuple-element.21.cout, ...), custom_call_target="tpu_custom_call" | custom-call | tf_op jit(solution)/shard_map/pallas_call | solution.py:687

commit v5 on v3

--- a/solution.py
+++ b/solution.py
@@ -163,7 +163,7 @@
            cout, fgrad, wf_grad, gf_grad, proj_grad, wc_grad, gc_grad, store_sem,
            field, cot, gain_f, wf, proj, gain_c, wc, load_sem,
            E, HF, X3f, PU, CI, HC, X3c, C, X3g, DC, D, X3d, T,
-           row_out, col_out, row_in, col_in, slots,
+           row_out, col_out, row_in, col_in, slots_f, slots_c,
            data_c, full_c, lc1, lc2, lc3, data_b, full_b, lb1, lb2, lb3, data_f, full_f, lf1, lf2, lf3,
            rim_send, rim_recv, sum_send, sum_recv, c_send, c_recv, b_send, b_recv, f_send, f_recv):
     H, W, h, w, wp, wpc, ngy, ngx = sizes
@@ -217,21 +217,24 @@
 
     each_peer(greet)
 
+    def slots_of(turn):
+        return (slots_c if turn in (1, 2) else slots_f).at[turn // 2]
+
     def sum_copy(turn, step):
         peer, device = peer_of(step)
+        slots = slots_of(turn)
         go = pltpu.make_async_remote_copy(
-            src_ref=slots.at[turn, me], dst_ref=slots.at[turn, me],
+            src_ref=slots.at[me], dst_ref=slots.at[me],
             send_sem=sum_send.at[step], recv_sem=sum_recv.at[turn % 2, me],
             device_id=device, device_id_type=MESH)
         come = pltpu.make_async_remote_copy(
-            src_ref=slots.at[turn, peer], dst_ref=slots.at[turn, peer],
+            src_ref=slots.at[peer], dst_ref=slots.at[peer],
             send_sem=sum_send.at[step], recv_sem=sum_recv.at[turn % 2, peer],
             device_id=device, device_id_type=MESH)
         return go, come
 
     def sums_start(turn, rows):
-        pad = jnp.zeros((8 - rows.shape[0], 128), F32)
-        slots[turn, me] = jnp.concatenate([rows, pad], axis=0)
+        slots_of(turn)[me] = rows
 
         each_peer(lambda step: sum_copy(turn, step)[0].start())
 
@@ -242,7 +245,7 @@
             come.wait_recv()
 
         each_peer(settle)
-        return jnp.sum(slots[turn], axis=0)
+        return jnp.sum(slots_of(turn)[...], axis=0)
 
     loads[0].wait()
     values = field[...].astype(F32)
@@ -349,7 +352,7 @@
 
     for number in (2, 3, 4, 5):
         loads[number].wait()
-    total = group_sums(sums_finish(0)[0:2], c1 // GROUPS)
+    total = group_sums(sums_finish(0), c1 // GROUPS)
     avg_f = total[0:1] / fine_count
     inv_f = lax.rsqrt(total[1:2] / fine_count - avg_f * avg_f + EPSILON)
     gain = gain_f[...]
@@ -520,7 +523,7 @@
     big.finish(2)
     big.start(3)
 
-    total = sums_finish(3)[0:2]
+    total = sums_finish(3)
     big.finish(3)
     big.start(4)
     small.finish(1)
@@ -638,7 +641,8 @@
         pltpu.VMEM((2, 3 * H + 4 * h, 128), BF16),
         pltpu.VMEM((8, 3 * wp + 4 * wpc, 128), BF16),
         pltpu.VMEM((2, 3 * H + 4 * h, 128), BF16),
-        pltpu.VMEM((4, everyone, 8, 128), F32),
+        pltpu.VMEM((2, everyone, 2, 128), F32),
+        pltpu.VMEM((2, everyone, 4, 128), F32),
         pltpu.VMEM((rows_c, 128), BF16), pltpu.VMEM((rows_c, 128), BF16), *landings(rows_c),
         pltpu.VMEM((rows_b, 128), BF16), pltpu.VMEM((rows_b, 128), BF16),
         *landings(rows_b, (2, ngy, ngx // 2)),

time: 65.5 us -> 61.3 us (0.936)
  Pallas kernels: 64.7 us -> 60.5 us
    pallas_call x1, Pallas kernels: 61.4 us -> 57.2 us  [on_device(): pl.pallas_call(functools.partial(kernel, sizes), out_shape=shapes(BF16),...]
where the time goes in v5:
time: 61.3 us; the launch traced here: 61.1 us
  Pallas kernels  60.5 us (99%)
  between operations  0.64 us (1%)
    pallas_call x1, Pallas kernels, on_device(): pl.pallas_call(functools.partial(kernel, sizes), out_shape=shapes(BF16),...  57.2 us
    pallas_call x1, Pallas kernels, on_device(): pl.pallas_call(deliver, out_shape=shapes(F32), in_specs=[hbm] * 7, out_sp...  3.31 us

profile of v5, /device:TPU:0, one launch (start us, length us, event | category | flops | bytes accessed | tf_op | source)
XLA Modules:
  0.0 61.1 jit_solution(7757213087744071771)
XLA Ops:
  0.6 57.2 %shard_map.126 = (bf16[32,8,256]{2,1,0:T(8,128)(2,1)}, bf16[64,16,128]{2,1,0:T(8,128)(2,1)}, bf16[1152,128]{1,0:T(8,128)(2,1)}, f32[1,128]{1,0:T(1,128)}, bf16[1...) custom-call(bf16[64,16,128]{2,1,0:T(8,128)(2,1)} %field_h.1, bf16[32,8,256]{2,1,0:T(8,128)(2,1)} %cot_h.1, ...), custom_call_target="tpu_custom_call" | custom-call | tf_op jit(solution)/shard_map/pallas_call | solution.py:666
  57.8 3.3 %shard_map.127 = (bf16[32,8,256]{2,1,0:T(8,128)(2,1)}, bf16[64,16,128]{2,1,0:T(8,128)(2,1)}, f32[1152,128]{1,0:T(8,128)}, f32[1,128]{1,0:T(1,128)}, f32[128,256]...) custom-call(bf16[32,8,256]{2,1,0:T(8,128)(2,1)} %get-tuple-element.21.cout, ...), custom_call_target="tpu_custom_call" | custom-call | tf_op jit(solution)/shard_map/pallas_call | solution.py:679
